TPU v7x, 128 devices: a whole 4x4x4 slice. The times are simulated.
128 devices in a mesh: ang: 16 (over x, y), sp: 8 (over z, core).
Axes of the slice: x: 4, y: 4, z: 4, core: 2. Of those that a mesh axis runs over, the one named last changes fastest.
Arguments:
- inputs: bfloat16 [16, 16, 4, 64, 192], P('ang', None, None, 'sp'), may hold values from -6 to 6
- cotangent: bfloat16 [16, 16, 4, 64, 192], P('ang', None, None, 'sp'), may hold values from -6 to 6
- kernel: bfloat16 [3, 3, 3, 3, 192, 192], replicated, may hold values from -0.046875 to 0.046875
- moment_one: float32 [2985984], P(('ang', 'sp')), may hold values from -3 to 3
- moment_two: float32 [2985984], P(('ang', 'sp')), may hold values from 0.05 to 1
Outputs:
- grad_input: bfloat16 [16, 16, 4, 64, 192], P('ang', None, None, 'sp')
- moment_next: float32 [2985984], P(('ang', 'sp'))
- square_next: float32 [2985984], P(('ang', 'sp'))
- direction: float32 [2985984], P(('ang', 'sp'))
All inputs are finite; a program needn't handle non-finite values.
Results may differ from a plain program's by a relative error of at most 0.0049.
Values may be sent and summed in bfloat16 or wider, within the bound.
A program may use at most 128 MiB of HBM per device.

v0:
```python
import functools
import math

import jax
import jax.numpy as jnp
from jax import lax
from jax.experimental import pallas as pl
from jax.experimental.pallas import tpu as pltpu
from jax.sharding import PartitionSpec as P

beta_one = 0.9
beta_two = 0.999
adam_step = 100
epsilon = 1e-08

MESH = pl.DeviceIdType.MESH
F32 = jnp.float32
BF16 = jnp.bfloat16

V, S, T, C = 16, 4, 8, 192
CELLS = V * S * T
GROUP = 9 * C
WIDE = GROUP + 64
ROWS = 9 * GROUP
LANES = 256
SIDES = ((0, 1), (0, -1), (1, 0), (-1, 0), (1, 1), (1, -1), (-1, 1), (-1, -1))


def start_halo(field, send, recv):
    rows, cols = lax.axis_size("ang"), lax.axis_size("sp")
    row, col = lax.axis_index("ang"), lax.axis_index("sp")
    jobs = []
    for side, (da, ds) in enumerate(SIDES):
        if ds == 0:
            src, dst = pl.ds(1, T), pl.ds(1, T)
        elif ds == 1:
            src, dst = pl.ds(T, 1), pl.ds(0, 1)
        else:
            src, dst = pl.ds(1, 1), pl.ds(T + 1, 1)
        sent = (row + da >= 0) & (row + da < rows) & (col + ds >= 0) & (col + ds < cols)
        got = (row - da >= 0) & (row - da < rows) & (col - ds >= 0) & (col - ds < cols)
        copy = pltpu.make_async_remote_copy(
            src_ref=field.at[1, pl.ds(1, S), src],
            dst_ref=field.at[1 - da, pl.ds(1, S), dst],
            send_sem=send.at[side],
            recv_sem=recv.at[side],
            device_id=(row + da, col + ds),
            device_id_type=MESH,
        )
        pl.when(sent)(copy.start)
        jobs.append((copy, sent, got))
    return jobs


def enter_halo():
    rows, cols = lax.axis_size("ang"), lax.axis_size("sp")
    row, col = lax.axis_index("ang"), lax.axis_index("sp")
    barrier = pltpu.get_barrier_semaphore()
    for da, ds in SIDES:
        there = (row + da >= 0) & (row + da < rows) & (col + ds >= 0) & (col + ds < cols)

        @pl.when(there)
        def _():
            pl.semaphore_signal(
                barrier, inc=1, device_id=(row + da, col + ds), device_id_type=MESH
            )

    tall = 1 + (row > 0).astype(jnp.int32) + (row < rows - 1).astype(jnp.int32)
    broad = 1 + (col > 0).astype(jnp.int32) + (col < cols - 1).astype(jnp.int32)
    pl.semaphore_wait(barrier, tall * broad - 1)


def unfold(field, taps, view_row):
    @pl.loop(0, S)
    def _(s):
        def low(k):
            block = field[view_row, s + k // 3, pl.ds(k % 3, T)]
            return block.reshape(T * V, LANES)

        out = pl.ds(pl.multiple_of(s * T * V, T * V), T * V)
        for pair in range(4):
            first = low(2 * pair)
            second = pltpu.roll(low(2 * pair + 1), 64, 1)
            at = 384 * pair
            taps[out, at : at + 128] = first[:, :128]
            taps[out, at + 128 : at + 256] = first[:, 128:] + second[:, :128]
            taps[out, at + 256 : at + 384] = second[:, 128:]
        taps[out, 1536:1792] = low(8)


def shifted(values, by):
    rows = values.shape[0]
    view = lax.broadcasted_iota(jnp.int32, values.shape, 0) % V
    keep = (view >= by) if by > 0 else (view < V + by)
    return jnp.where(keep, pltpu.roll(values, by % rows, 0), jnp.zeros_like(values))


def correlate(taps, weights, acc, view_row, first):
    @pl.loop(0, 3)
    def _(b):
        at = pl.multiple_of((view_row * 3 + b) * GROUP, 64)
        term = jnp.dot(taps[...], weights[pl.ds(at, WIDE), :], preferred_element_type=F32)
        if first:
            acc[b] = term
        else:
            acc[b] += term


def forward_kernel(x_ref, cot_ref, w_ref, dw_ref, gp_ref, xp, xc, wv, acc, gall, send, recv, wsem):
    rest = pl.ds(ROWS, WIDE - GROUP)
    wcopy = pltpu.make_async_copy(w_ref, wv.at[pl.ds(0, ROWS)], wsem)
    wcopy.start()
    wv[rest, :] = jnp.zeros((WIDE - GROUP, C), BF16)
    xp[...] = jnp.zeros_like(xp)
    gp_ref[...] = jnp.zeros_like(gp_ref)
    for s in range(S):
        block = jnp.swapaxes(x_ref[0, :, s].astype(F32), 0, 1).astype(BF16)
        xp[1, 1 + s, 1 : 1 + T, :, 0:C] = block
    enter_halo()
    jobs = start_halo(xp, send.at[0], recv.at[0])
    for copy, _, got in jobs:
        pl.when(got)(copy.wait_recv)
    wcopy.wait()
    for view_row in range(3):
        unfold(xp, xc.at[view_row], view_row)
    for view_row in (1, 0, 2):
        correlate(xc.at[view_row], wv, acc, view_row, view_row == 1)
    for copy, sent, _ in jobs:
        pl.when(sent)(copy.wait_send)

    preact = shifted(acc[0], 1) + acc[1] + shifted(acc[2], -1)
    for s in range(S):
        upstream = jnp.swapaxes(cot_ref[0, :, s].astype(F32), 0, 1).reshape(T * V, C)
        pre = preact[s * T * V : (s + 1) * T * V]
        sigmoid = jax.nn.sigmoid(pre)
        grad = upstream * sigmoid * (1.0 + pre * (1.0 - sigmoid))
        gp_ref[1, 1 + s, 1 : 1 + T, :, 0:C] = grad.astype(BF16).reshape(T, V, C)
    jobs = start_halo(gp_ref, send.at[1], recv.at[1])
    grad = gp_ref[1, 1 : 1 + S, 1 : 1 + T].reshape(CELLS, LANES)
    wide = grad.astype(F32)
    gall[:, 0:256] = shifted(wide, -1).astype(BF16)
    gall[:, 256:512] = grad
    gall[:, 512:768] = shifted(wide, 1).astype(BF16)

    for a in range(3):
        for part in range(5):
            at, size = 384 * part, (384 if part < 4 else 192)
            term = lax.dot_general(
                xc[a, :, at : at + (size if part < 4 else 256)],
                gall[...],
                (((0,), (0,)), ((), ())),
                preferred_element_type=F32,
            )
            for b in range(3):
                row = (3 * a + b) * GROUP + at
                dw_ref[row : row + size, :] = term[0:size, 256 * b : 256 * b + C].astype(BF16)

    for copy, sent, got in jobs:
        pl.when(sent)(copy.wait_send)
        pl.when(got)(copy.wait_recv)


def input_kernel(gp_ref, w_ref, out_ref, wv, wt, gc, acc, wsem):
    wcopy = pltpu.make_async_copy(w_ref, wv, wsem)
    wcopy.start()
    wt[pl.ds(ROWS, WIDE - GROUP), :] = jnp.zeros((WIDE - GROUP, C), BF16)
    wcopy.wait()

    @pl.loop(0, 81)
    def _(tap):
        src = pl.ds(pl.multiple_of((80 - tap) * C, 64), C)
        dst = pl.ds(pl.multiple_of(tap * C, 64), C)
        wt[dst, :] = wv[src, :].T

    for view_row in range(3):
        unfold(gp_ref, gc.at[view_row], view_row)
    for view_row in (1, 0, 2):
        correlate(gc.at[view_row], wt, acc, view_row, view_row == 1)
    total = shifted(acc[0], 1) + acc[1] + shifted(acc[2], -1)
    for s in range(S):
        block = total[s * T * V : (s + 1) * T * V].reshape(T, V, C)
        out_ref[0, :, s] = jnp.swapaxes(block, 0, 1).astype(BF16)


def local(inputs, cotangent, kernel, moment_one, moment_two):
    flat = kernel.reshape(ROWS, C)
    vmem = pl.BlockSpec(memory_space=pltpu.VMEM)
    anywhere = pl.BlockSpec(memory_space=pl.ANY)
    padded = (3, S + 2, T + 2, V, LANES)
    params = functools.partial(pltpu.CompilerParams, vmem_limit_bytes=56 * 1024 * 1024)
    terms, grads = pl.pallas_call(
        forward_kernel,
        out_shape=(
            jax.ShapeDtypeStruct((ROWS, C), BF16),
            jax.ShapeDtypeStruct(padded, BF16),
        ),
        in_specs=[vmem, vmem, anywhere],
        out_specs=(vmem, vmem),
        scratch_shapes=[
            pltpu.VMEM(padded, BF16),
            pltpu.VMEM((3, CELLS, WIDE), BF16),
            pltpu.VMEM((ROWS + WIDE - GROUP, C), BF16),
            pltpu.VMEM((3, CELLS, C), F32),
            pltpu.VMEM((CELLS, 768), BF16),
            pltpu.SemaphoreType.DMA((2, 8)),
            pltpu.SemaphoreType.DMA((2, 8)),
            pltpu.SemaphoreType.DMA,
        ],
        compiler_params=params(collective_id=0, has_side_effects=True),
        cost_estimate=pl.CostEstimate(flops=6 * 10**9, bytes_accessed=16 * 10**6, transcendentals=10**5),
    )(inputs, cotangent, flat)
    grad_input = pl.pallas_call(
        input_kernel,
        out_shape=jax.ShapeDtypeStruct(inputs.shape, BF16),
        in_specs=[vmem, anywhere],
        out_specs=vmem,
        scratch_shapes=[
            pltpu.VMEM((ROWS, C), BF16),
            pltpu.VMEM((ROWS + WIDE - GROUP, C), BF16),
            pltpu.VMEM((3, CELLS, WIDE), BF16),
            pltpu.VMEM((3, CELLS, C), F32),
            pltpu.SemaphoreType.DMA,
        ],
        compiler_params=params(),
        cost_estimate=pl.CostEstimate(flops=3 * 10**9, bytes_accessed=10**7, transcendentals=0),
    )(grads, flat)
    share = lax.psum_scatter(terms.reshape(-1), ("ang", "sp"), scatter_dimension=0, tiled=True)
    pixels = CELLS * lax.axis_size("ang") * lax.axis_size("sp")
    grad_share = share.astype(F32) * F32(1.0 / math.sqrt(pixels))
    moment_next = beta_one * moment_one + (1.0 - beta_one) * grad_share
    square_next = beta_two * moment_two + (1.0 - beta_two) * grad_share * grad_share
    first_fix = 1.0 - beta_one**adam_step
    second_fix = 1.0 - beta_two**adam_step
    direction = moment_next / first_fix / (jnp.sqrt(square_next / second_fix) + epsilon)
    return (grad_input, moment_next, square_next, direction)


def solution(mesh):
    field = P("ang", None, None, "sp", None)
    share = P(("ang", "sp"))
    return jax.shard_map(
        local,
        mesh=mesh,
        in_specs=(field, field, P(), share, share),
        out_specs=(field, share, share, share),
        check_vma=False,
    )
```

profile of v0, /device:TPU:1, one launch (start us, length us, event | category | flops | bytes accessed | tf_op | source)
XLA Modules:
  0.0 226.2 jit_solution(5341356413595981246)
XLA Ops:
  7.2 0.0 all-reduce.3.cloned.1.call-start
  7.2 36.9 %shard_map.84 = (bf16[15552,192]{1,0:T(8,128)(2,1)}, bf16[3,6,10,16,256]{4,3,2,1,0:T(8,128)(2,1)}) custom-call(bf16[1,16,4,8,192]{4,3,2,1,0:T(8,128)(2,1)} %x_ref.1, bf16[1,16,4,8,192]{4,3,2,1,0:T(8,128)(2,1)} %cot_ref.1, bf16[15552,192]{1,0:T(8,128)(2,1)} %bitcast.1), custom_call_target="tpu_custom_call" | custom-call | flops 6000000000 | bytes 16000000 | tf_op jit(solution)/shard_map/pallas_call | solution.py:191
  44.1 14.8 %reshape.15 = bf16[2985984]{0:T(1024)(128)(2,1)} reshape(bf16[15552,192]{1,0:T(8,128)(2,1)} %get-tuple-element.7) | data formatting | bytes 11943936 | tf_op jit(solution)/shard_map/reshape | solution.py:227
  58.9 0.0 all-reduce.3.cloned.1.call-update
  58.9 0.0 copy-start
  59.0 0.0 copy-start.1
  59.0 19.7 %shard_map.85 = bf16[1,16,4,8,192]{4,3,2,1,0:T(8,128)(2,1)} custom-call(bf16[3,6,10,16,256]{4,3,2,1,0:T(8,128)(2,1)} %get-tuple-element.6.gp_ref, bf16[15552,192]{1,0:T(8,128)(2,1)} %bitcast.2), custom_call_target="tpu_custom_call" | custom-call | flops 3000000000 | bytes 10000000 | tf_op jit(solution)/shard_map/pallas_call | solution.py:212
  78.7 139.1 %all-reduce.3.cloned.1.call-done = bf16[2985984]{0:T(1024)(128)(2,1)} async-done(((bf16[2985984]{0:T(1024)(128)(2,1)}), bf16[2985984]{0:T(1024)(128)(2,1)}) %all-reduce.3.cloned.1.call-update) | async-done | bytes 5971984
  217.7 0.0 copy-done
  217.8 0.0 copy-done.1
  217.8 1.6 add_divide_fusion
Async XLA Ops:
  7.2 210.6 %all-reduce.3.cloned.1.call-start = ((), (), s32[]{:S(2)}) async-start(), calls=%async_computation | async-start | bytes 11943936
  58.9 158.8 %copy-start = (f32[23328]{0:T(1024)S(1)}, f32[23328]{0:T(1024)}, u32[]{:S(2)}) copy-start(f32[23328]{0:T(1024)} %param.9) | copy-start | bytes 279940
  59.0 158.8 %copy-start.1 = (f32[23328]{0:T(1024)S(1)}, f32[23328]{0:T(1024)}, u32[]{:S(2)}) copy-start(f32[23328]{0:T(1024)} %param.8) | copy-start | bytes 279940
Sparse Core Ops, SparseCore 0:
  59.1 158.6 all-reduce.2
where the time goes:
time: 227 us; the launch traced here: 226 us
  waiting for transfers between devices  139 us (61%)
  Pallas kernels  56.6 us (25%)
  local copies, waits for them, and re-layouts  14.8 us (7%)
  between operations  14.1 us (6%)
    unnamed x2, waiting for transfers between devices  139 us
    pallas_call x1, Pallas kernels, local(): pl.pallas_call(forward_kernel, out_shape=(jax.ShapeDtypeStruct((ROWS, C),...  36.9 us
    pallas_call x1, Pallas kernels, local(): pl.pallas_call(input_kernel, out_shape=jax.ShapeDtypeStruct(inputs.shape,...  19.7 us
    reshape x1, local copies, waits for them, and re-layouts, local(): terms.reshape(-1)  14.8 us
  transfers between devices with their start and end apart: 1, of which 1 were waited for; matrix products, arithmetic and copies ran while one was open for 0% of the time, Pallas kernels for 9%

commit v1 on v0

v1 whole, which is shorter than its diff:
```python
import functools
import math

import jax
import jax.numpy as jnp
from jax import lax
from jax.experimental import pallas as pl
from jax.experimental.pallas import tpu as pltpu
from jax.sharding import PartitionSpec as P

beta_one = 0.9
beta_two = 0.999
adam_step = 100
epsilon = 1e-08

MESH = pl.DeviceIdType.MESH
F32 = jnp.float32
BF16 = jnp.bfloat16

V, S, T, C = 16, 4, 8, 192
CELLS = V * S * T
GROUP = 9 * C
WIDE = GROUP + 64
ROWS = 9 * GROUP
LANES = 256
SIDES = ((0, 1), (0, -1), (1, 0), (-1, 0), (1, 1), (1, -1), (-1, 1), (-1, -1))


def start_halo(field, send, recv):
    rows, cols = lax.axis_size("ang"), lax.axis_size("sp")
    row, col = lax.axis_index("ang"), lax.axis_index("sp")
    jobs = []
    for side, (da, ds) in enumerate(SIDES):
        if ds == 0:
            src, dst = pl.ds(1, T), pl.ds(1, T)
        elif ds == 1:
            src, dst = pl.ds(T, 1), pl.ds(0, 1)
        else:
            src, dst = pl.ds(1, 1), pl.ds(T + 1, 1)
        sent = (row + da >= 0) & (row + da < rows) & (col + ds >= 0) & (col + ds < cols)
        got = (row - da >= 0) & (row - da < rows) & (col - ds >= 0) & (col - ds < cols)
        copy = pltpu.make_async_remote_copy(
            src_ref=field.at[1, pl.ds(1, S), src],
            dst_ref=field.at[1 - da, pl.ds(1, S), dst],
            send_sem=send.at[side],
            recv_sem=recv.at[side],
            device_id=(row + da, col + ds),
            device_id_type=MESH,
        )
        pl.when(sent)(copy.start)
        jobs.append((copy, sent, got))
    return jobs


def enter():
    rows, cols = lax.axis_size("ang"), lax.axis_size("sp")
    row, col = lax.axis_index("ang"), lax.axis_index("sp")
    barrier = pltpu.get_barrier_semaphore()

    def greet(peer):
        pl.semaphore_signal(barrier, inc=1, device_id=peer, device_id_type=MESH)

    for da, ds in SIDES:
        there = (row + da >= 0) & (row + da < rows) & (col + ds >= 0) & (col + ds < cols)
        pl.when(there)(functools.partial(greet, (row + da, col + ds)))
    for axis in range(3):
        for step in range(1, 4):
            greet(peer_along(axis, step))
    greet(sibling())
    tall = 1 + (row > 0).astype(jnp.int32) + (row < rows - 1).astype(jnp.int32)
    broad = 1 + (col > 0).astype(jnp.int32) + (col < cols - 1).astype(jnp.int32)
    pl.semaphore_wait(barrier, tall * broad + 9)


def place():
    row, col = lax.axis_index("ang"), lax.axis_index("sp")
    return lax.div(row, 4), lax.rem(row, 4), lax.div(col, 2), lax.rem(col, 2)


def peer_along(axis, step):
    at = list(place())
    at[axis] = lax.rem(at[axis] + step, 4)
    return (at[0] * 4 + at[1], at[2] * 2 + at[3])


def sibling():
    x, y, z, core = place()
    return (x * 4 + y, z * 2 + 1 - core)


def unfold(field, taps, view_row):
    @pl.loop(0, S)
    def _(s):
        def low(k):
            block = field[view_row, s + k // 3, pl.ds(k % 3, T)]
            return block.reshape(T * V, LANES)

        out = pl.ds(pl.multiple_of(s * T * V, T * V), T * V)
        for pair in range(4):
            first = low(2 * pair)
            second = pltpu.roll(low(2 * pair + 1), 64, 1)
            at = 384 * pair
            taps[out, at : at + 128] = first[:, :128]
            taps[out, at + 128 : at + 256] = first[:, 128:] + second[:, :128]
            taps[out, at + 256 : at + 384] = second[:, 128:]
        taps[out, 1536:1792] = low(8)


def shifted(values, by):
    rows = values.shape[0]
    view = lax.broadcasted_iota(jnp.int32, values.shape, 0) % V
    keep = (view >= by) if by > 0 else (view < V + by)
    return jnp.where(keep, pltpu.roll(values, by % rows, 0), jnp.zeros_like(values))


def correlate(taps, weights, acc, view_row, first):
    @pl.loop(0, 3)
    def _(b):
        at = pl.multiple_of((view_row * 3 + b) * GROUP, 64)
        term = jnp.dot(taps[...], weights[pl.ds(at, WIDE), :], preferred_element_type=F32)
        if first:
            acc[b] = term
        else:
            acc[b] += term


UNITS = 243
TILE = (16, 128)
HALVES = (32, 36, 40)
HALVES_NEXT = (9, 10, 10)


def window(chips, index, count):
    start = (index * (chips * 243)) // 64
    if isinstance(index, int):
        return min(start, UNITS - count)
    return jnp.minimum(start, UNITS - count)


def kernel_terms(taps, grads, dw, a):
    for part in range(5):
        at, size = 384 * part, (384 if part < 4 else 192)
        term = lax.dot_general(
            taps[a, :, at : at + (size if part < 4 else 256)],
            grads[...],
            (((0,), (0,)), ((), ())),
            preferred_element_type=F32,
        )
        for b in range(3):
            count = size // 64
            block = term[0:size, 256 * b : 256 * b + 256].reshape(count, 2, 2, 16, 256)
            dst = pl.ds((3 * a + b) * 27 + 6 * part, count)
            for core in range(2):
                low, high = block[:, core, 0], block[:, core, 1]
                dw[core, 0, dst] = low[:, :, :128].astype(BF16)
                dw[core, 1, dst] = high[:, :, :128].astype(BF16)
                tail = pltpu.roll(high[:, :, 128:].reshape(count * 16, 128), 64, 1)
                dw[core, 2, dst] = (low[:, :, 128:] + tail.reshape(count, 16, 128)).astype(BF16)


def send_to(peer, src, dst, sems, index):
    copy = pltpu.make_async_remote_copy(
        src_ref=src,
        dst_ref=dst,
        send_sem=sems.at[0, index],
        recv_sem=sems.at[1, index],
        device_id=peer,
        device_id_type=MESH,
    )
    copy.start()
    return copy


class Ring:
    def __init__(self, axis, src, got, relay, sems):
        self.axis, self.src, self.got, self.relay, self.sems = axis, src, got, relay, sems
        self.me = place()[axis]
        self.up, self.across, self.down = (lax.rem(self.me + k, 4) for k in (1, 2, 3))

    def send(self, src, slot):
        peer = peer_along(self.axis, 1 if slot % 2 == 0 else 3)
        return send_to(peer, src, self.got.at[slot], self.sems, slot)

    def open(self):
        src = self.src
        self.jobs = [self.send(src.at[self.across, 1 - k], k) for k in range(2)]
        self.jobs.append(self.send(src.at[self.up, 0], 2))
        self.jobs.append(self.send(src.at[self.down, 1], 3))

    def pass_on(self):
        self.jobs[0].wait_recv()
        self.relay[0] = self.got[0] + self.src[self.up, 1]
        self.jobs.append(self.send(self.relay.at[0], 4))
        self.jobs[1].wait_recv()
        self.relay[1] = self.got[1] + self.src[self.down, 0]
        self.jobs.append(self.send(self.relay.at[1], 5))

    def close(self):
        for job in self.jobs[2:]:
            job.wait_recv()
        for job in self.jobs:
            job.wait_send()
        wide = lambda tile: tile.astype(F32)
        first = wide(self.src[self.me, 0]) + wide(self.got[2]) + wide(self.got[5])
        second = wide(self.src[self.me, 1]) + wide(self.got[3]) + wide(self.got[4])
        return first.astype(BF16), second.astype(BF16)


def step_kernel(
    x_ref, cot_ref, w_ref, gi_ref, gk_ref,
    xp, gp, xc, wv, wt, acc, gall, dw, pair,
    first_a, first_b, first_c, got_a, got_b, got_c, relay_a, relay_b, relay_c,
    sum_a, sum_b, sum_c,
    second_a, second_b, second_c, next_a, next_b, next_c, pass_a, pass_b, pass_c,
    last_a, last_b, last_c, ends, both,
    halo_send, halo_recv, wsem, pair_sems, ring_sems, next_sems, last_sems, core_sems,
):
    chip_x, chip_y, chip_z, core = place()
    wcopy = pltpu.make_async_copy(w_ref, wv.at[pl.ds(0, ROWS)], wsem)
    wcopy.start()
    xp[...] = jnp.zeros_like(xp)
    gp[...] = jnp.zeros_like(gp)
    for s in range(S):
        block = jnp.swapaxes(x_ref[0, :, s].astype(F32), 0, 1).astype(BF16)
        xp[1, 1 + s, 1 : 1 + T, :, 0:C] = block
    enter()
    jobs = start_halo(xp, halo_send.at[0], halo_recv.at[0])

    rest = pl.ds(ROWS, WIDE - GROUP)
    wv[rest, :] = jnp.zeros((WIDE - GROUP, C), BF16)
    wt[rest, :] = jnp.zeros((WIDE - GROUP, C), BF16)
    wcopy.wait()

    @pl.loop(0, 81)
    def _(tap):
        src = pl.ds(pl.multiple_of((80 - tap) * C, 64), C)
        dst = pl.ds(pl.multiple_of(tap * C, 64), C)
        wt[dst, :] = wv[src, :].T

    for copy, _, got in jobs:
        pl.when(got)(copy.wait_recv)
    for copy, sent, _ in jobs:
        pl.when(sent)(copy.wait_send)
    for view_row in range(3):
        unfold(xp, xc.at[view_row], view_row)
    for view_row in (1, 0, 2):
        correlate(xc.at[view_row], wv, acc, view_row, view_row == 1)

    preact = shifted(acc[0], 1) + acc[1] + shifted(acc[2], -1)
    for s in range(S):
        upstream = jnp.swapaxes(cot_ref[0, :, s].astype(F32), 0, 1).reshape(T * V, C)
        pre = preact[s * T * V : (s + 1) * T * V]
        sigmoid = jax.nn.sigmoid(pre)
        grad = upstream * sigmoid * (1.0 + pre * (1.0 - sigmoid))
        gp[1, 1 + s, 1 : 1 + T, :, 0:C] = grad.astype(BF16).reshape(T, V, C)
    jobs = start_halo(gp, halo_send.at[1], halo_recv.at[1])
    grad = gp[1, 1 : 1 + S, 1 : 1 + T].reshape(CELLS, LANES)
    wide = grad.astype(F32)
    gall[:, 0:256] = shifted(wide, -1).astype(BF16)
    gall[:, 256:512] = grad
    gall[:, 512:768] = shifted(wide, 1).astype(BF16)

    pairs = []
    for a in range(3):
        kernel_terms(xc, gall, dw, a)
        units = pl.ds(81 * a, 81)
        src, dst = dw.at[1 - core, :, units], pair.at[:, units]
        pairs.append(send_to(sibling(), src, dst, pair_sems, a))

    for copy, sent, got in jobs:
        pl.when(got)(copy.wait_recv)
    for copy, sent, got in jobs:
        pl.when(sent)(copy.wait_send)
    for view_row in range(3):
        unfold(gp, xc.at[view_row], view_row)
    for copy in pairs:
        copy.wait()

    def both_cores(plane, start, count):
        units = pl.ds(start, count)
        return dw[core, plane, units] + pair[plane, units]

    for x in range(4):
        for half in range(2):
            first_a[x, half] = both_cores(0, window(16, x, 64) + 32 * half, 32)

    @pl.loop(0, 16)
    def _(xy):
        x, y = xy // 4, xy % 4
        first_b[y, x // 2, pl.ds((x % 2) * 18, 18)] = both_cores(1, window(4, xy, 18), 18)

    @pl.loop(0, 64)
    def _(q):
        x, y, z = q // 16, (q // 4) % 4, q % 4
        to = ((x % 2) * 4 + y) * 5
        first_c[z, x // 2, pl.ds(to, 5)] = both_cores(2, window(1, q, 5), 5)

    rings = [
        Ring(0, first_a, got_a, relay_a, ring_sems.at[0]),
        Ring(1, first_b, got_b, relay_b, ring_sems.at[1]),
        Ring(2, first_c, got_c, relay_c, ring_sems.at[2]),
    ]
    for ring in rings:
        ring.open()
    correlate(xc.at[1], wt, acc, 1, True)
    correlate(xc.at[0], wt, acc, 0, False)
    for ring in rings:
        ring.pass_on()
    correlate(xc.at[2], wt, acc, 2, False)

    column = chip_x * 4 + chip_y
    chip = column * 4 + chip_z
    low, high = rings[0].close()
    sum_a[0:32] = low
    sum_a[32:64] = high
    for y in range(4):
        start = window(4, chip_x * 4 + y, 18) - window(16, chip_x, 64)
        for half in range(2):
            second_a[y, half] = sum_a[pl.ds(start + 9 * half, 9)]
    low, high = rings[1].close()
    sum_b[0:2] = low.reshape(2, 18, *TILE)
    sum_b[2:4] = high.reshape(2, 18, *TILE)
    for x in range(4):
        for z in range(4):
            start = window(1, x * 16 + chip_y * 4 + z, 5) - window(4, x * 4 + chip_y, 18)
            second_b[z, x // 2, 5 * (x % 2) : 5 * (x % 2) + 5] = sum_b[x, pl.ds(start, 5)]
    low, high = rings[2].close()
    second_c[0:2] = low.reshape(2, 2, 10, *TILE)
    second_c[2:4] = high.reshape(2, 2, 10, *TILE)

    rings = [
        Ring(1, second_a, next_a, pass_a, next_sems.at[0]),
        Ring(2, second_b, next_b, pass_b, next_sems.at[1]),
        Ring(0, second_c, next_c, pass_c, next_sems.at[2]),
    ]
    for ring in rings:
        ring.open()
    total = shifted(acc[0], 1) + acc[1] + shifted(acc[2], -1)
    for s in range(S):
        block = total[s * T * V : (s + 1) * T * V].reshape(T, V, C)
        gi_ref[0, :, s] = jnp.swapaxes(block, 0, 1).astype(BF16)
    for ring in rings:
        ring.pass_on()
    low, high = rings[0].close()
    last = []
    sum_a[0:9] = low
    sum_a[9:18] = high
    for z in range(4):
        start = window(1, column * 4 + z, 5) - window(4, column, 18)
        last_a[z] = sum_a[pl.ds(start, 5)]
    low, high = rings[1].close()
    last_b[0:2] = low.reshape(2, 5, *TILE)
    last_b[2:4] = high.reshape(2, 5, *TILE)
    low, high = rings[2].close()
    last_c[0:2] = low.reshape(2, 5, *TILE)
    last_c[2:4] = high.reshape(2, 5, *TILE)

    jobs = []
    for plane, (axis, src) in enumerate(((2, last_a), (0, last_b), (1, last_c))):
        for step in range(1, 4):
            target = lax.rem(place()[axis] + step, 4)
            slot = 3 * plane + step - 1
            jobs.append(send_to(peer_along(axis, step), src.at[target], ends.at[slot], last_sems, slot))
    for job in jobs:
        job.wait()
    for plane, (me, src) in enumerate(((chip_z, last_a), (chip_x, last_b), (chip_y, last_c))):
        total = src[me].astype(F32)
        for step in range(3):
            total += ends[3 * plane + step].astype(F32)
        both[core, plane] = total
    send_to(sibling(), both.at[core], both.at[core], core_sems, 0).wait()
    for k in range(2):
        gk_ref[:, k, 0, :, 0:128] = both[k, 0]
        gk_ref[:, k, 1, :, 0:128] = both[k, 1]
        tail = both[k, 2]
        gk_ref[:, k, 0, :, 128:192] = tail[:, :, 0:64]
        turned = pltpu.roll(tail.reshape(80, 128), 64, 1).reshape(5, 16, 128)
        gk_ref[:, k, 1, :, 128:192] = turned[:, :, 0:64]


def local(inputs, cotangent, kernel, moment_one, moment_two):
    vmem = pl.BlockSpec(memory_space=pltpu.VMEM)
    anywhere = pl.BlockSpec(memory_space=pl.ANY)
    padded = (3, S + 2, T + 2, V, LANES)
    tiles = lambda *lead: pltpu.VMEM((*lead, *TILE), BF16)
    dma = lambda *shape: pltpu.SemaphoreType.DMA(shape)
    long_kernel = pltpu.VMEM((ROWS + WIDE - GROUP, C), BF16)
    grad_input, window_grad = pl.pallas_call(
        step_kernel,
        out_shape=(
            jax.ShapeDtypeStruct(inputs.shape, BF16),
            jax.ShapeDtypeStruct((5, 2, 2, 16, C), F32),
        ),
        in_specs=[vmem, vmem, anywhere],
        out_specs=(vmem, vmem),
        scratch_shapes=[
            pltpu.VMEM(padded, BF16),
            pltpu.VMEM(padded, BF16),
            pltpu.VMEM((3, CELLS, WIDE), BF16),
            long_kernel,
            long_kernel,
            pltpu.VMEM((3, CELLS, C), F32),
            pltpu.VMEM((CELLS, 768), BF16),
            tiles(2, 3, UNITS),
            tiles(3, UNITS),
            *(tiles(4, 2, n) for n in HALVES),
            *(tiles(6, n) for n in HALVES),
            *(tiles(2, n) for n in HALVES),
            tiles(64),
            tiles(4, 18),
            tiles(4, 2, 10),
            *(tiles(4, 2, n) for n in HALVES_NEXT),
            *(tiles(6, n) for n in HALVES_NEXT),
            *(tiles(2, n) for n in HALVES_NEXT),
            *(tiles(4, 5) for _ in range(3)),
            tiles(9, 5),
            pltpu.VMEM((2, 3, 5, *TILE), F32),
            dma(2, 8),
            dma(2, 8),
            pltpu.SemaphoreType.DMA,
            dma(2, 3),
            dma(3, 2, 6),
            dma(3, 2, 6),
            dma(2, 9),
            dma(2, 1),
        ],
        compiler_params=pltpu.CompilerParams(
            vmem_limit_bytes=56 * 1024 * 1024, collective_id=0, has_side_effects=True
        ),
        cost_estimate=pl.CostEstimate(flops=9 * 10**9, bytes_accessed=10**7, transcendentals=10**5),
    )(inputs, cotangent, kernel.reshape(ROWS, C))
    share_len = moment_one.shape[0]
    chip = lax.axis_index("ang") * 4 + lax.axis_index("sp") // 2
    device = lax.axis_index(("ang", "sp"))
    begin = device * share_len - window(1, chip, 5) * (64 * C)
    share = lax.dynamic_slice_in_dim(window_grad.reshape(-1), begin, share_len, 0)
    pixels = CELLS * lax.axis_size("ang") * lax.axis_size("sp")
    grad_share = share * F32(1.0 / math.sqrt(pixels))
    moment_next = beta_one * moment_one + (1.0 - beta_one) * grad_share
    square_next = beta_two * moment_two + (1.0 - beta_two) * grad_share * grad_share
    first_fix = 1.0 - beta_one**adam_step
    second_fix = 1.0 - beta_two**adam_step
    direction = moment_next / first_fix / (jnp.sqrt(square_next / second_fix) + epsilon)
    return (grad_input, moment_next, square_next, direction)


def solution(mesh):
    field = P("ang", None, None, "sp", None)
    share = P(("ang", "sp"))
    return jax.shard_map(
        local,
        mesh=mesh,
        in_specs=(field, field, P(), share, share),
        out_specs=(field, share, share, share),
        check_vma=False,
    )
```

time: 227 us -> 73.5 us (0.32)
  waiting for transfers between devices: 139 us -> 0 us
  between operations: 14.1 us -> 0.72 us
  Pallas kernels: 56.6 us -> 68.9 us
  local copies, waits for them, and re-layouts: 14.8 us -> 2.83 us
    unnamed x2 -> x0, waiting for transfers between devices: 139 us -> none
    reshape x1, local copies, waits for them, and re-layouts: 14.8 us -> 1.15 us  [local(): window_grad.reshape(-1)]
    pallas_call x2 -> x1, Pallas kernels: 56.6 us -> 68.9 us  [local(): pl.pallas_call(step_kernel, out_shape=(jax.ShapeDtypeStruct(inputs.shape,...]
  transfers between devices with their start and end apart: 1 -> 0, of which waited for: 1 -> 0; matrix products, arithmetic and copies ran while one was open for 0% -> 0% of each run, Pallas kernels for 9% -> 0%
where the time goes in v1:
time: 73.5 us; the launch traced here: 73.3 us
  Pallas kernels  68.9 us (94%)
  local copies, waits for them, and re-layouts  2.83 us (4%)
  other arithmetic  0.83 us (1%)
    pallas_call x1, Pallas kernels, local(): pl.pallas_call(step_kernel, out_shape=(jax.ShapeDtypeStruct(inputs.shape,...  68.9 us
    unnamed x5, local copies, waits for them, and re-layouts  1.68 us

profile of v1, /device:TPU:1, one launch (start us, length us, event | category | flops | bytes accessed | tf_op | source)
XLA Modules:
  0.0 73.3 jit_solution(8180746731183289448)
XLA Ops:
  0.7 0.0 copy-start
  0.7 0.0 copy-start.1
  0.7 68.9 %shard_map.84 = (bf16[1,16,4,8,192]{4,3,2,1,0:T(8,128)(2,1)}, f32[5,2,2,16,192]{4,3,2,1,0:T(8,128)}) custom-call(bf16[1,16,4,8,192]{4,3,2,1,0:T(8,128)(2,1)} %x_ref.1, bf16[1,16,4,8,192]{4,3,2,1,0:T(8,128)(2,1)} %cot_ref.1, bf16[15552,192]{1,0:T(8,128)(2,1)} %bitcast.3), custom_call_target="tpu_custom_call" | custom-call | flops 8999999488 | bytes 10000000 | tf_op jit(solution)/shard_map/pallas_call | solution.py:388
  69.6 1.1 %reshape.15 = f32[61440]{0:T(1024)S(1)} reshape(f32[5,2,2,16,192]{4,3,2,1,0:T(8,128)} %get-tuple-element.7) | data formatting | bytes 491520 | tf_op jit(solution)/shard_map/reshape | solution.py:436
  70.8 0.0 copy-done
  70.8 0.0 copy-done.1
  70.8 0.8 %add_divide_fusion = (f32[23328]{0:T(1024)}, f32[23328]{0:T(1024)}, f32[23328]{0:T(1024)}) fusion(f32[61440]{0:T(1024)S(1)} %reshape.15, s32[]{:T(128)S(6)} %select_n.13, f32[23328]{0:T(1024)S(1)} %copy-done, f32[23328]{0:T(1024)S(1)} %copy-done.1), kind=kLoop, calls=%fused_computation | loop fusion | flops 279936 | bytes 559876 | tf_op jit(solution)/shard_map/div | solution.py:443
  71.6 1.7 %copy.10 = bf16[1,16,4,8,192]{4,3,2,1,0:T(8,128)(2,1)} copy(bf16[1,16,4,8,192]{4,3,2,1,0:T(8,128)(2,1)} %get-tuple-element.15) | data formatting | bytes 393216
Async XLA Ops:
  0.7 70.1 %copy-start = (f32[23328]{0:T(1024)S(1)}, f32[23328]{0:T(1024)}, u32[]{:S(2)}) copy-start(f32[23328]{0:T(1024)} %param.9) | copy-start | bytes 279940
  0.7 70.1 %copy-start.1 = (f32[23328]{0:T(1024)S(1)}, f32[23328]{0:T(1024)}, u32[]{:S(2)}) copy-start(f32[23328]{0:T(1024)} %param.8) | copy-start | bytes 279940

commit v2 on v1

v2 whole, which is shorter than its diff:
```python
import functools
import math

import jax
import jax.numpy as jnp
from jax import lax
from jax.experimental import pallas as pl
from jax.experimental.pallas import tpu as pltpu
from jax.sharding import PartitionSpec as P

beta_one = 0.9
beta_two = 0.999
adam_step = 100
epsilon = 1e-08

MESH = pl.DeviceIdType.MESH
F32 = jnp.float32
BF16 = jnp.bfloat16

V, S, T, C = 16, 4, 8, 192
CELLS = V * S * T
GROUP = 9 * C
WIDE = GROUP + 64
ROWS = 9 * GROUP
LANES = 256
SIDES = ((0, 1), (0, -1), (1, 0), (-1, 0), (1, 1), (1, -1), (-1, 1), (-1, -1))


def start_halo(field, send, recv):
    rows, cols = lax.axis_size("ang"), lax.axis_size("sp")
    row, col = lax.axis_index("ang"), lax.axis_index("sp")
    jobs = []
    for side, (da, ds) in enumerate(SIDES):
        if ds == 0:
            src, dst = pl.ds(1, T), pl.ds(1, T)
        elif ds == 1:
            src, dst = pl.ds(T, 1), pl.ds(0, 1)
        else:
            src, dst = pl.ds(1, 1), pl.ds(T + 1, 1)
        sent = (row + da >= 0) & (row + da < rows) & (col + ds >= 0) & (col + ds < cols)
        got = (row - da >= 0) & (row - da < rows) & (col - ds >= 0) & (col - ds < cols)
        copy = pltpu.make_async_remote_copy(
            src_ref=field.at[1, pl.ds(1, S), src],
            dst_ref=field.at[1 - da, pl.ds(1, S), dst],
            send_sem=send.at[side],
            recv_sem=recv.at[side],
            device_id=(row + da, col + ds),
            device_id_type=MESH,
        )
        pl.when(sent)(copy.start)
        jobs.append((copy, sent, got))
    return jobs


def greet():
    rows, cols = lax.axis_size("ang"), lax.axis_size("sp")
    row, col = lax.axis_index("ang"), lax.axis_index("sp")
    barrier = pltpu.get_barrier_semaphore()

    def signal(peer):
        pl.semaphore_signal(barrier, inc=1, device_id=peer, device_id_type=MESH)

    for da, ds in SIDES:
        there = (row + da >= 0) & (row + da < rows) & (col + ds >= 0) & (col + ds < cols)
        pl.when(there)(functools.partial(signal, (row + da, col + ds)))
    for axis in range(3):
        for step in range(1, 4):
            signal(peer_along(axis, step))
    signal(sibling())
    tall = 1 + (row > 0).astype(jnp.int32) + (row < rows - 1).astype(jnp.int32)
    broad = 1 + (col > 0).astype(jnp.int32) + (col < cols - 1).astype(jnp.int32)
    return tall * broad + 9


def place():
    row, col = lax.axis_index("ang"), lax.axis_index("sp")
    return lax.div(row, 4), lax.rem(row, 4), lax.div(col, 2), lax.rem(col, 2)


def device(at):
    return (at[0] * 4 + at[1], at[2] * 2 + at[3])


def peer_along(axis, step):
    at = list(place())
    at[axis] = lax.rem(at[axis] + step, 4)
    return device(at)


def sibling():
    x, y, z, core = place()
    return (x * 4 + y, z * 2 + 1 - core)


def unfold(field, taps, view_row):
    @pl.loop(0, S)
    def _(s):
        def low(k):
            block = field[view_row, s + k // 3, pl.ds(k % 3, T)]
            return block.reshape(T * V, LANES)

        out = pl.ds(pl.multiple_of(s * T * V, T * V), T * V)
        for pair in range(4):
            first = low(2 * pair)
            second = pltpu.roll(low(2 * pair + 1), 64, 1)
            at = 384 * pair
            taps[out, at : at + 128] = first[:, :128]
            taps[out, at + 128 : at + 256] = first[:, 128:] + second[:, :128]
            taps[out, at + 256 : at + 384] = second[:, 128:]
        taps[out, 1536:1792] = low(8)


def shifted(values, by):
    rows = values.shape[0]
    view = lax.broadcasted_iota(jnp.int32, values.shape, 0) % V
    keep = (view >= by) if by > 0 else (view < V + by)
    return jnp.where(keep, pltpu.roll(values, by % rows, 0), jnp.zeros_like(values))


def correlate(taps, weights, acc, view_row, first):
    @pl.loop(0, 3)
    def _(b):
        at = pl.multiple_of((view_row * 3 + b) * GROUP, 64)
        term = jnp.dot(taps[...], weights[pl.ds(at, WIDE), :], preferred_element_type=F32)
        if first:
            acc[b] = term
        else:
            acc[b] += term


UNITS = 243
TILE = (16, 128)
LENGTHS = (64, 72, 80)


def window(chips, index, count):
    start = (index * (chips * 243)) // 64
    if isinstance(index, int):
        return min(start, UNITS - count)
    return jnp.minimum(start, UNITS - count)


def kernel_terms(taps, grads, dw, a):
    for part in range(5):
        at, size = 384 * part, (384 if part < 4 else 192)
        term = lax.dot_general(
            taps[a, :, at : at + (size if part < 4 else 256)],
            grads[...],
            (((0,), (0,)), ((), ())),
            preferred_element_type=F32,
        )
        for b in range(3):
            count = size // 64
            block = term[0:size, 256 * b : 256 * b + 256].reshape(count, 2, 2, 16, 256)
            dst = pl.ds((3 * a + b) * 27 + 6 * part, count)
            for core in range(2):
                low, high = block[:, core, 0], block[:, core, 1]
                dw[core, 0, dst] = low[:, :, :128].astype(BF16)
                dw[core, 1, dst] = high[:, :, :128].astype(BF16)
                tail = pltpu.roll(high[:, :, 128:].reshape(count * 16, 128), 64, 1)
                dw[core, 2, dst] = (low[:, :, 128:] + tail.reshape(count, 16, 128)).astype(BF16)


def send_to(peer, src, dst, sems, index):
    copy = pltpu.make_async_remote_copy(
        src_ref=src,
        dst_ref=dst,
        send_sem=sems.at[0, index],
        recv_sem=sems.at[1, index],
        device_id=peer,
        device_id_type=MESH,
    )
    copy.start()
    return copy


def pieces(plane):
    if plane == 0:
        found = []
        for x in range(4):
            start = window(16, x, 64)
            for a in range(3):
                low, high = max(start, 81 * a), min(start + 64, 81 * a + 81)
                if low < high:
                    found.append((x, low - start, low, high - low))
        return found
    if plane == 1:
        return [(p % 4, 18 * (p // 4), window(4, p, 18), 18) for p in range(16)]
    return [(q % 4, 5 * (q // 4), window(1, q, 5), 5) for q in range(64)]


def ready(start, count):
    return (start + count - 1) // 81


def spans(plane):
    found = {}
    for target, at, start, count in pieces(plane):
        key = (target, ready(start, count))
        low, size = found.get(key, (at, 0))
        found[key] = (low, size + count)
    return found


class Scatter:
    def __init__(self, plane, terms, got, send, recv):
        self.axis, self.terms, self.got, self.send, self.recv = plane, terms, got, send, recv
        self.me = place()[plane]
        self.spans = spans(plane)

    def copy(self, target, a, slot):
        low, size = self.spans[target, a]
        at = list(place())
        at[self.axis] = target
        return pltpu.make_async_remote_copy(
            src_ref=self.terms.at[target, pl.ds(low, size)],
            dst_ref=self.got.at[slot, pl.ds(low, size)],
            send_sem=self.send.at[target, a],
            recv_sem=self.recv.at[slot, a],
            device_id=device(at),
            device_id_type=MESH,
        )

    def start(self, now):
        for target, a in self.spans:
            if a == now:
                slot = lax.rem(self.me + 3 - target, 4)

                @pl.when(self.me != target)
                def _():
                    self.copy(target, a, slot).start()

    def wait(self):
        for target, a in self.spans:

            @pl.when(self.me == target)
            def _():
                for slot in range(3):
                    self.copy(target, a, slot).wait_recv()

        for target, a in self.spans:

            @pl.when(self.me != target)
            def _():
                self.copy(target, a, 0).wait_send()

    def total(self, units):
        value = self.terms[self.me, units].astype(F32)
        for slot in range(3):
            value += self.got[slot, units].astype(F32)
        return value.astype(BF16)


def step_kernel(
    x_ref, cot_ref, w_ref, gi_ref, gk_ref,
    xp, gp, xc, wv, wt, acc, gall, dw, pair,
    first_a, first_b, first_c, got_a, got_b, got_c, sum_a, sum_b, sum_c, ends, both,
    halo_send, halo_recv, wsem, pair_sems, first_send, first_recv, last_sems, core_sems,
):
    chip_x, chip_y, chip_z, core = place()
    wcopy = pltpu.make_async_copy(w_ref, wv.at[pl.ds(0, ROWS)], wsem)
    wcopy.start()
    xp[...] = jnp.zeros_like(xp)
    peers = greet()
    for s in range(S):
        block = jnp.swapaxes(x_ref[0, :, s].astype(F32), 0, 1).astype(BF16)
        xp[1, 1 + s, 1 : 1 + T, :, 0:C] = block
    gp[...] = jnp.zeros_like(gp)
    rest = pl.ds(ROWS, WIDE - GROUP)
    wv[rest, :] = jnp.zeros((WIDE - GROUP, C), BF16)
    wt[rest, :] = jnp.zeros((WIDE - GROUP, C), BF16)
    pl.semaphore_wait(pltpu.get_barrier_semaphore(), peers)
    jobs = start_halo(xp, halo_send.at[0], halo_recv.at[0])

    wcopy.wait()

    @pl.loop(0, 81)
    def _(tap):
        src = pl.ds(pl.multiple_of((80 - tap) * C, 64), C)
        dst = pl.ds(pl.multiple_of(tap * C, 64), C)
        wt[dst, :] = wv[src, :].T

    for copy, _, got in jobs[:2]:
        pl.when(got)(copy.wait_recv)
    unfold(xp, xc.at[1], 1)
    correlate(xc.at[1], wv, acc, 1, True)
    for copy, _, got in jobs[2:]:
        pl.when(got)(copy.wait_recv)
    for view_row in (0, 2):
        unfold(xp, xc.at[view_row], view_row)
        correlate(xc.at[view_row], wv, acc, view_row, False)
    for copy, sent, _ in jobs:
        pl.when(sent)(copy.wait_send)

    preact = shifted(acc[0], 1) + acc[1] + shifted(acc[2], -1)
    for s in range(S):
        upstream = jnp.swapaxes(cot_ref[0, :, s].astype(F32), 0, 1).reshape(T * V, C)
        pre = preact[s * T * V : (s + 1) * T * V]
        sigmoid = jax.nn.sigmoid(pre)
        grad = upstream * sigmoid * (1.0 + pre * (1.0 - sigmoid))
        gp[1, 1 + s, 1 : 1 + T, :, 0:C] = grad.astype(BF16).reshape(T, V, C)
    jobs = start_halo(gp, halo_send.at[1], halo_recv.at[1])
    grad = gp[1, 1 : 1 + S, 1 : 1 + T].reshape(CELLS, LANES)
    wide = grad.astype(F32)
    gall[:, 0:256] = shifted(wide, -1).astype(BF16)
    gall[:, 256:512] = grad
    gall[:, 512:768] = shifted(wide, 1).astype(BF16)

    firsts = (first_a, first_b, first_c)
    scatters = [
        Scatter(k, firsts[k], (got_a, got_b, got_c)[k], first_send.at[k], first_recv.at[k])
        for k in range(3)
    ]

    def exchange(a):
        units = pl.ds(81 * a, 81)
        return send_to(sibling(), dw.at[1 - core, :, units], pair.at[:, units], pair_sems, a)

    def both_cores(plane, start, count):
        units = pl.ds(start, count)
        return dw[core, plane, units] + pair[plane, units]

    def scatter(copy, a):
        copy.wait_recv()
        for plane in range(2):
            for target, at, start, count in pieces(plane):
                if ready(start, count) == a:
                    firsts[plane][target, at : at + count] = both_cores(plane, start, count)
            scatters[plane].start(a)
        chips = [q for q, (_, _, start, count) in enumerate(pieces(2)) if ready(start, count) == a]

        @pl.loop(chips[0], chips[-1] + 1)
        def _(q):
            at = pl.ds((q // 4) * 5, 5)
            first_c[q % 4, at] = both_cores(2, window(1, q, 5), 5)

        scatters[2].start(a)

    kernel_terms(xc, gall, dw, 0)
    pairs = [exchange(0)]
    for a in (1, 2):
        kernel_terms(xc, gall, dw, a)
        pairs.append(exchange(a))
        scatter(pairs[a - 1], a - 1)
    scatter(pairs[2], 2)

    for copy, sent, got in jobs:
        pl.when(got)(copy.wait_recv)
    for view_row in (1, 0, 2):
        unfold(gp, xc.at[view_row], view_row)
        correlate(xc.at[view_row], wt, acc, view_row, view_row == 1)

    for ring in scatters:
        ring.wait()
    sum_a[...] = scatters[0].total(pl.ds(0, 64))
    for x in range(4):
        sum_b[x] = scatters[1].total(pl.ds(18 * x, 18))

    @pl.loop(0, 16)
    def _(p):
        sum_c[p] = scatters[2].total(pl.ds(5 * p, 5))

    def chip_at(plane, step):
        at = [chip_x, chip_y, chip_z, core]
        for axis, ahead in zip(((1, 2), (0, 2), (0, 1))[plane], (step // 4, step % 4)):
            at[axis] = lax.rem(at[axis] + ahead, 4)
        return at

    def part(plane, at):
        column = at[0] * 4 + at[1]
        start = window(1, column * 4 + at[2], 5)
        if plane == 0:
            return sum_a.at[pl.ds(start - window(16, at[0], 64), 5)]
        if plane == 1:
            return sum_b.at[at[0], pl.ds(start - window(4, column, 18), 5)]
        return sum_c.at[column]

    def last(plane, step):
        at = chip_at(plane, step)
        return pltpu.make_async_remote_copy(
            src_ref=part(plane, at),
            dst_ref=ends.at[plane, step],
            send_sem=last_sems.at[0, plane, step],
            recv_sem=last_sems.at[1, plane, step],
            device_id=device(at),
            device_id_type=MESH,
        )

    @pl.loop(1, 16)
    def _(step):
        for plane in range(3):
            last(plane, step).start()

    total = shifted(acc[0], 1) + acc[1] + shifted(acc[2], -1)
    for s in range(S):
        block = total[s * T * V : (s + 1) * T * V].reshape(T, V, C)
        gi_ref[0, :, s] = jnp.swapaxes(block, 0, 1).astype(BF16)
    for copy, sent, got in jobs:
        pl.when(sent)(copy.wait_send)
    for copy in pairs:
        copy.wait_send()

    for plane in range(3):
        both[core, plane] = part(plane, chip_at(plane, 0))[...].astype(F32)

    @pl.loop(1, 16)
    def _(step):
        for plane in range(3):
            last(plane, step).wait()
            both[core, plane] += ends[plane, step].astype(F32)

    send_to(sibling(), both.at[core], both.at[core], core_sems, 0).wait()
    for k in range(2):
        gk_ref[:, k, 0, :, 0:128] = both[k, 0]
        gk_ref[:, k, 1, :, 0:128] = both[k, 1]
        tail = both[k, 2]
        gk_ref[:, k, 0, :, 128:192] = tail[:, :, 0:64]
        turned = pltpu.roll(tail.reshape(80, 128), 64, 1).reshape(5, 16, 128)
        gk_ref[:, k, 1, :, 128:192] = turned[:, :, 0:64]


def local(inputs, cotangent, kernel, moment_one, moment_two):
    vmem = pl.BlockSpec(memory_space=pltpu.VMEM)
    anywhere = pl.BlockSpec(memory_space=pl.ANY)
    padded = (3, S + 2, T + 2, V, LANES)
    tiles = lambda *lead: pltpu.VMEM((*lead, *TILE), BF16)
    dma = lambda *shape: pltpu.SemaphoreType.DMA(shape)
    long_kernel = pltpu.VMEM((ROWS + WIDE - GROUP, C), BF16)
    grad_input, window_grad = pl.pallas_call(
        step_kernel,
        out_shape=(
            jax.ShapeDtypeStruct(inputs.shape, BF16),
            jax.ShapeDtypeStruct((5, 2, 2, 16, C), F32),
        ),
        in_specs=[vmem, vmem, anywhere],
        out_specs=(vmem, vmem),
        scratch_shapes=[
            pltpu.VMEM(padded, BF16),
            pltpu.VMEM(padded, BF16),
            pltpu.VMEM((3, CELLS, WIDE), BF16),
            long_kernel,
            long_kernel,
            pltpu.VMEM((3, CELLS, C), F32),
            pltpu.VMEM((CELLS, 768), BF16),
            tiles(2, 3, UNITS),
            tiles(3, UNITS),
            *(tiles(4, n) for n in LENGTHS),
            *(tiles(3, n) for n in LENGTHS),
            tiles(64),
            tiles(4, 18),
            tiles(16, 5),
            tiles(3, 16, 5),
            pltpu.VMEM((2, 3, 5, *TILE), F32),
            dma(2, 8),
            dma(2, 8),
            pltpu.SemaphoreType.DMA,
            dma(2, 3),
            dma(3, 4, 3),
            dma(3, 3, 3),
            dma(2, 3, 16),
            dma(2, 1),
        ],
        compiler_params=pltpu.CompilerParams(
            vmem_limit_bytes=56 * 1024 * 1024, collective_id=0, has_side_effects=True
        ),
        cost_estimate=pl.CostEstimate(flops=9 * 10**9, bytes_accessed=10**7, transcendentals=10**5),
    )(inputs, cotangent, kernel.reshape(ROWS, C))
    share_len = moment_one.shape[0]
    chip = lax.axis_index("ang") * 4 + lax.axis_index("sp") // 2
    begin = lax.axis_index(("ang", "sp")) * share_len - window(1, chip, 5) * (64 * C)
    share = lax.dynamic_slice_in_dim(window_grad.reshape(-1), begin, share_len, 0)
    pixels = CELLS * lax.axis_size("ang") * lax.axis_size("sp")
    grad_share = share * F32(1.0 / math.sqrt(pixels))
    moment_next = beta_one * moment_one + (1.0 - beta_one) * grad_share
    square_next = beta_two * moment_two + (1.0 - beta_two) * grad_share * grad_share
    first_fix = 1.0 - beta_one**adam_step
    second_fix = 1.0 - beta_two**adam_step
    direction = moment_next / first_fix / (jnp.sqrt(square_next / second_fix) + epsilon)
    return (grad_input, moment_next, square_next, direction)


def solution(mesh):
    field = P("ang", None, None, "sp", None)
    share = P(("ang", "sp"))
    return jax.shard_map(
        local,
        mesh=mesh,
        in_specs=(field, field, P(), share, share),
        out_specs=(field, share, share, share),
        check_vma=False,
    )
```

time: 73.5 us -> 66.7 us (0.907)
  Pallas kernels: 68.9 us -> 62.1 us
    pallas_call x1, Pallas kernels: 68.9 us -> 62.1 us  [local(): pl.pallas_call(step_kernel, out_shape=(jax.ShapeDtypeStruct(inputs.shape,...]
where the time goes in v2:
time: 66.7 us; the launch traced here: 66.5 us
  Pallas kernels  62.1 us (93%)
  local copies, waits for them, and re-layouts  2.83 us (4%)
  other arithmetic  0.83 us (1%)
  between operations  0.72 us (1%)
    pallas_call x1, Pallas kernels, local(): pl.pallas_call(step_kernel, out_shape=(jax.ShapeDtypeStruct(inputs.shape,...  62.1 us
    unnamed x5, local copies, waits for them, and re-layouts  1.68 us

profile of v2, /device:TPU:1, one launch (start us, length us, event | category | flops | bytes accessed | tf_op | source)
XLA Modules:
  0.0 66.5 jit_solution(3283152945475487351)
XLA Ops:
  0.7 0.0 copy-start
  0.7 0.0 copy-start.1
  0.7 62.1 %shard_map.84 = (bf16[1,16,4,8,192]{4,3,2,1,0:T(8,128)(2,1)}, f32[5,2,2,16,192]{4,3,2,1,0:T(8,128)}) custom-call(bf16[1,16,4,8,192]{4,3,2,1,0:T(8,128)(2,1)} %x_ref.1, bf16[1,16,4,8,192]{4,3,2,1,0:T(8,128)(2,1)} %cot_ref.1, bf16[15552,192]{1,0:T(8,128)(2,1)} %bitcast.3), custom_call_target="tpu_custom_call" | custom-call | flops 8999999488 | bytes 10000000 | tf_op jit(solution)/shard_map/pallas_call | solution.py:429
  62.9 1.1 %reshape.15 = f32[61440]{0:T(1024)S(1)} reshape(f32[5,2,2,16,192]{4,3,2,1,0:T(8,128)} %get-tuple-element.7) | data formatting | bytes 491520 | tf_op jit(solution)/shard_map/reshape | solution.py:471
  64.0 0.0 copy-done
  64.0 0.0 copy-done.1
  64.0 0.8 %add_divide_fusion = (f32[23328]{0:T(1024)}, f32[23328]{0:T(1024)}, f32[23328]{0:T(1024)}) fusion(f32[61440]{0:T(1024)S(1)} %reshape.15, s32[]{:T(128)S(6)} %select_n.13, f32[23328]{0:T(1024)S(1)} %copy-done, f32[23328]{0:T(1024)S(1)} %copy-done.1), kind=kLoop, calls=%fused_computation | loop fusion | flops 279936 | bytes 559876 | tf_op jit(solution)/shard_map/div | solution.py:478
  64.9 1.7 %copy.10 = bf16[1,16,4,8,192]{4,3,2,1,0:T(8,128)(2,1)} copy(bf16[1,16,4,8,192]{4,3,2,1,0:T(8,128)(2,1)} %get-tuple-element.15) | data formatting | bytes 393216
Async XLA Ops:
  0.7 63.3 %copy-start = (f32[23328]{0:T(1024)S(1)}, f32[23328]{0:T(1024)}, u32[]{:S(2)}) copy-start(f32[23328]{0:T(1024)} %param.9) | copy-start | bytes 279940
  0.7 63.3 %copy-start.1 = (f32[23328]{0:T(1024)S(1)}, f32[23328]{0:T(1024)}, u32[]{:S(2)}) copy-start(f32[23328]{0:T(1024)} %param.8) | copy-start | bytes 279940

commit v3 on v2

--- a/solution.py
+++ b/solution.py
@@ -254,8 +254,9 @@
 def step_kernel(
     x_ref, cot_ref, w_ref, gi_ref, gk_ref,
     xp, gp, xc, wv, wt, acc, gall, dw, pair,
-    first_a, first_b, first_c, got_a, got_b, got_c, sum_a, sum_b, sum_c, ends, both,
-    halo_send, halo_recv, wsem, pair_sems, first_send, first_recv, last_sems, core_sems,
+    first_a, first_b, first_c, got_a, got_b, got_c, sum_a, sum_b, sum_c,
+    next_b, near_a, near_b, near_c, last_a, last_b, last_c, ends, both, left, right,
+    halo_send, halo_recv, wsem, pair_sems, first_send, first_recv, next_sems, last_sems, core_sems,
 ):
     chip_x, chip_y, chip_z, core = place()
     wcopy = pltpu.make_async_copy(w_ref, wv.at[pl.ds(0, ROWS)], wsem)
@@ -336,19 +337,23 @@
 
         scatters[2].start(a)
 
+    def input_terms(view_row, first):
+        unfold(gp, xc.at[view_row], view_row)
+        correlate(xc.at[view_row], wt, acc, view_row, first)
+
     kernel_terms(xc, gall, dw, 0)
     pairs = [exchange(0)]
     for a in (1, 2):
         kernel_terms(xc, gall, dw, a)
         pairs.append(exchange(a))
         scatter(pairs[a - 1], a - 1)
+    for copy, _, got in jobs[:2]:
+        pl.when(got)(copy.wait_recv)
+    input_terms(1, True)
     scatter(pairs[2], 2)
-
-    for copy, sent, got in jobs:
+    for copy, _, got in jobs[2:]:
         pl.when(got)(copy.wait_recv)
-    for view_row in (1, 0, 2):
-        unfold(gp, xc.at[view_row], view_row)
-        correlate(xc.at[view_row], wt, acc, view_row, view_row == 1)
+    input_terms(0, False)
 
     for ring in scatters:
         ring.wait()
@@ -358,65 +363,85 @@
 
     @pl.loop(0, 16)
     def _(p):
-        sum_c[p] = scatters[2].total(pl.ds(5 * p, 5))
-
-    def chip_at(plane, step):
-        at = [chip_x, chip_y, chip_z, core]
-        for axis, ahead in zip(((1, 2), (0, 2), (0, 1))[plane], (step // 4, step % 4)):
-            at[axis] = lax.rem(at[axis] + ahead, 4)
-        return at
-
-    def part(plane, at):
-        column = at[0] * 4 + at[1]
-        start = window(1, column * 4 + at[2], 5)
+        sum_c[p // 4, p % 4] = scatters[2].total(pl.ds(5 * p, 5))
+
+    chips = (chip_x, chip_y, chip_z)
+    column = chip_x * 4 + chip_y
+
+    def next_part(plane, to):
         if plane == 0:
-            return sum_a.at[pl.ds(start - window(16, at[0], 64), 5)]
-        if plane == 1:
-            return sum_b.at[at[0], pl.ds(start - window(4, column, 18), 5)]
-        return sum_c.at[column]
-
-    def last(plane, step):
-        at = chip_at(plane, step)
-        return pltpu.make_async_remote_copy(
-            src_ref=part(plane, at),
-            dst_ref=ends.at[plane, step],
-            send_sem=last_sems.at[0, plane, step],
-            recv_sem=last_sems.at[1, plane, step],
-            device_id=device(at),
-            device_id_type=MESH,
-        )
-
-    @pl.loop(1, 16)
-    def _(step):
-        for plane in range(3):
-            last(plane, step).start()
-
+            return sum_a.at[pl.ds(window(4, chip_x * 4 + to, 18) - window(16, chip_x, 64), 18)]
+        return (next_b if plane == 1 else sum_c).at[to]
+
+    for x in range(4):
+        for z in range(4):
+            start = window(1, x * 16 + chip_y * 4 + z, 5) - window(4, x * 4 + chip_y, 18)
+            next_b[z, x] = sum_b[x, pl.ds(start, 5)]
+    sends = []
+    for step in (2, 1, 3):
+        for plane, axis in enumerate((1, 2, 0)):
+            src = next_part(plane, lax.rem(chips[axis] + step, 4))
+            dst = (near_a, near_b, near_c)[plane].at[step - 1]
+            sends.append(send_to(peer_along(axis, step), src, dst, next_sems.at[plane], step - 1))
+
+    input_terms(2, False)
     total = shifted(acc[0], 1) + acc[1] + shifted(acc[2], -1)
     for s in range(S):
         block = total[s * T * V : (s + 1) * T * V].reshape(T, V, C)
         gi_ref[0, :, s] = jnp.swapaxes(block, 0, 1).astype(BF16)
-    for copy, sent, got in jobs:
+
+    for copy in sends:
+        copy.wait_recv()
+
+    def near_total(plane, near):
+        value = next_part(plane, chips[(1, 2, 0)[plane]])[...].astype(F32)
+        for k in range(3):
+            value += near[k].astype(F32)
+        return value.astype(BF16)
+
+    last_a[...] = near_total(0, near_a)
+    last_b[...] = near_total(1, near_b)
+    last_c[...] = near_total(2, near_c)
+
+    def last_part(plane, to):
+        if plane == 0:
+            return last_a.at[pl.ds(window(1, column * 4 + to, 5) - window(4, column, 18), 5)]
+        return (last_b if plane == 1 else last_c).at[to]
+
+    lasts = []
+    for step in (2, 1, 3):
+        for plane, axis in enumerate((2, 0, 1)):
+            src = last_part(plane, lax.rem(chips[axis] + step, 4))
+            slot = 3 * plane + step - 1
+            lasts.append(send_to(peer_along(axis, step), src, ends.at[slot], last_sems, slot))
+    for copy, sent, _ in jobs:
         pl.when(sent)(copy.wait_send)
-    for copy in pairs:
+    for copy in (*pairs, *sends):
         copy.wait_send()
-
-    for plane in range(3):
-        both[core, plane] = part(plane, chip_at(plane, 0))[...].astype(F32)
-
-    @pl.loop(1, 16)
-    def _(step):
-        for plane in range(3):
-            last(plane, step).wait()
-            both[core, plane] += ends[plane, step].astype(F32)
-
+    for copy in lasts:
+        copy.wait()
+    for plane, axis in enumerate((2, 0, 1)):
+        value = last_part(plane, chips[axis])[...].astype(F32)
+        for k in range(3):
+            value += ends[3 * plane + k].astype(F32)
+        both[core, plane] = value
     send_to(sibling(), both.at[core], both.at[core], core_sems, 0).wait()
+
     for k in range(2):
-        gk_ref[:, k, 0, :, 0:128] = both[k, 0]
-        gk_ref[:, k, 1, :, 0:128] = both[k, 1]
-        tail = both[k, 2]
-        gk_ref[:, k, 0, :, 128:192] = tail[:, :, 0:64]
-        turned = pltpu.roll(tail.reshape(80, 128), 64, 1).reshape(5, 16, 128)
-        gk_ref[:, k, 1, :, 128:192] = turned[:, :, 0:64]
+        for unit in range(5):
+            row = 64 * unit + 32 * k
+            tail = both[k, 2, unit]
+            left[row : row + 16] = both[k, 0, unit]
+            left[row + 16 : row + 32] = both[k, 1, unit]
+            right[row : row + 16] = tail
+            right[row + 16 : row + 32] = pltpu.roll(tail, 64, 1)
+    count = 160
+    odd = pltpu.roll(left[pl.ds(1, count, stride=2), :], 64, 1)
+    head = lax.broadcasted_iota(jnp.int32, (count, 128), 1) < 64
+    gk_ref[pl.ds(0, count, stride=3), :] = left[pl.ds(0, count, stride=2), :]
+    gk_ref[pl.ds(1, count, stride=3), :] = jnp.where(head, right[pl.ds(0, count, stride=2), :], odd)
+    rest = pltpu.roll(right[pl.ds(1, count, stride=2), :], 64, 1)
+    gk_ref[pl.ds(2, count, stride=3), :] = jnp.where(head, odd, rest)
 
 
 def local(inputs, cotangent, kernel, moment_one, moment_two):
@@ -430,7 +455,7 @@
         step_kernel,
         out_shape=(
             jax.ShapeDtypeStruct(inputs.shape, BF16),
-            jax.ShapeDtypeStruct((5, 2, 2, 16, C), F32),
+            jax.ShapeDtypeStruct((480, 128), F32),
         ),
         in_specs=[vmem, vmem, anywhere],
         out_specs=(vmem, vmem),
@@ -448,16 +473,26 @@
             *(tiles(3, n) for n in LENGTHS),
             tiles(64),
             tiles(4, 18),
-            tiles(16, 5),
-            tiles(3, 16, 5),
+            tiles(4, 4, 5),
+            tiles(4, 4, 5),
+            tiles(3, 18),
+            tiles(3, 4, 5),
+            tiles(3, 4, 5),
+            tiles(18),
+            tiles(4, 5),
+            tiles(4, 5),
+            tiles(9, 5),
             pltpu.VMEM((2, 3, 5, *TILE), F32),
+            pltpu.VMEM((320, 128), F32),
+            pltpu.VMEM((320, 128), F32),
             dma(2, 8),
             dma(2, 8),
             pltpu.SemaphoreType.DMA,
             dma(2, 3),
             dma(3, 4, 3),
             dma(3, 3, 3),
-            dma(2, 3, 16),
+            dma(3, 2, 3),
+            dma(2, 9),
             dma(2, 1),
         ],
         compiler_params=pltpu.CompilerParams(

time: 66.7 us -> 65.1 us (0.976)
  Pallas kernels: 62.1 us -> 60.8 us
  local copies, waits for them, and re-layouts: 2.83 us -> 1.68 us
  other arithmetic: 0.83 us -> 1.73 us
    pallas_call x1, Pallas kernels: 62.1 us -> 60.8 us  [local(): pl.pallas_call(step_kernel, out_shape=(jax.ShapeDtypeStruct(inputs.shape,...]
    reshape x1 -> x0, local copies, waits for them, and re-layouts: 1.15 us -> none  [local(): window_grad.reshape(-1)]
    div x1, other arithmetic: 0.83 us -> 1.73 us  [local(): moment_next / first_fix / (jnp.sqrt(square_next / second_fix) + epsilon)]
where the time goes in v3:
time: 65.1 us; the launch traced here: 64.9 us
  Pallas kernels  60.8 us (93%)
  other arithmetic  1.73 us (3%)
  local copies, waits for them, and re-layouts  1.68 us (3%)
  between operations  0.72 us (1%)
    pallas_call x1, Pallas kernels, local(): pl.pallas_call(step_kernel, out_shape=(jax.ShapeDtypeStruct(inputs.shape,...  60.8 us
    div x1, other arithmetic, local(): moment_next / first_fix / (jnp.sqrt(square_next / second_fix) + epsilon)  1.73 us
    unnamed x5, local copies, waits for them, and re-layouts  1.68 us

profile of v3, /device:TPU:1, one launch (start us, length us, event | category | flops | bytes accessed | tf_op | source)
XLA Modules:
  0.0 64.9 jit_solution(5216540364796327708)
XLA Ops:
  0.7 0.0 copy-start
  0.7 0.0 copy-start.1
  0.7 60.8 %shard_map.84 = (bf16[1,16,4,8,192]{4,3,2,1,0:T(8,128)(2,1)}, f32[480,128]{1,0:T(8,128)}) custom-call(bf16[1,16,4,8,192]{4,3,2,1,0:T(8,128)(2,1)} %x_ref.1, bf16[1,16,4,8,192]{4,3,2,1,0:T(8,128)(2,1)} %cot_ref.1, bf16[15552,192]{1,0:T(8,128)(2,1)} %bitcast.3), custom_call_target="tpu_custom_call" | custom-call | flops 8999999488 | bytes 10000000 | tf_op jit(solution)/shard_map/pallas_call | solution.py:454
  61.5 0.0 copy-done
  61.5 0.0 copy-done.1
  61.5 1.7 %add_divide_fusion = (f32[23328]{0:T(1024)}, f32[23328]{0:T(1024)}, f32[23328]{0:T(1024)}) fusion(f32[61440]{0:T(1024)} %bitcast.2, s32[]{:T(128)S(6)} %select_n.13, f32[23328]{0:T(1024)S(1)} %copy-done, f32[23328]{0:T(1024)S(1)} %copy-done.1), kind=kLoop, calls=%fused_computation | loop fusion | flops 279936 | bytes 559876 | tf_op jit(solution)/shard_map/div | solution.py:513
  63.3 1.7 %copy.10 = bf16[1,16,4,8,192]{4,3,2,1,0:T(8,128)(2,1)} copy(bf16[1,16,4,8,192]{4,3,2,1,0:T(8,128)(2,1)} %get-tuple-element.15) | data formatting | bytes 393216
Async XLA Ops:
  0.7 60.8 %copy-start = (f32[23328]{0:T(1024)S(1)}, f32[23328]{0:T(1024)}, u32[]{:S(2)}) copy-start(f32[23328]{0:T(1024)} %param.9) | copy-start | bytes 279940
  0.7 60.8 %copy-start.1 = (f32[23328]{0:T(1024)S(1)}, f32[23328]{0:T(1024)}, u32[]{:S(2)}) copy-start(f32[23328]{0:T(1024)} %param.8) | copy-start | bytes 279940

commit v4 on v3

--- a/solution.py
+++ b/solution.py
@@ -26,30 +26,57 @@
 SIDES = ((0, 1), (0, -1), (1, 0), (-1, 0), (1, 1), (1, -1), (-1, 1), (-1, -1))
 
 
-def start_halo(field, send, recv):
+def start_halo(field, packed, edges, rows_in, cols_in, send, recv):
     rows, cols = lax.axis_size("ang"), lax.axis_size("sp")
     row, col = lax.axis_index("ang"), lax.axis_index("sp")
+    for j in range(2):
+        first = field[1, 1 + 2 * j, 1 : 1 + T].reshape(T * V, LANES)
+        second = pltpu.roll(field[1, 2 + 2 * j, 1 : 1 + T].reshape(T * V, LANES), 64, 1)
+        packed[j, :, :, 0:128] = first[:, :128].reshape(T, V, 128)
+        packed[j, :, :, 128:256] = (first[:, 128:] + second[:, :128]).reshape(T, V, 128)
+        packed[j, :, :, 256:384] = second[:, 128:].reshape(T, V, 128)
+        edges[0, j] = packed[j, 0]
+        edges[1, j] = packed[j, T - 1]
     jobs = []
     for side, (da, ds) in enumerate(SIDES):
         if ds == 0:
-            src, dst = pl.ds(1, T), pl.ds(1, T)
+            src, dst = packed, rows_in.at[(1 - da) // 2]
         elif ds == 1:
-            src, dst = pl.ds(T, 1), pl.ds(0, 1)
+            src, dst = edges.at[1], cols_in.at[1 - da, 0]
         else:
-            src, dst = pl.ds(1, 1), pl.ds(T + 1, 1)
+            src, dst = edges.at[0], cols_in.at[1 - da, 1]
         sent = (row + da >= 0) & (row + da < rows) & (col + ds >= 0) & (col + ds < cols)
         got = (row - da >= 0) & (row - da < rows) & (col - ds >= 0) & (col - ds < cols)
         copy = pltpu.make_async_remote_copy(
-            src_ref=field.at[1, pl.ds(1, S), src],
-            dst_ref=field.at[1 - da, pl.ds(1, S), dst],
+            src_ref=src,
+            dst_ref=dst,
             send_sem=send.at[side],
             recv_sem=recv.at[side],
             device_id=(row + da, col + ds),
             device_id_type=MESH,
         )
-        pl.when(sent)(copy.start)
         jobs.append((copy, sent, got))
+    for side in (4, 5, 6, 7, 2, 3, 0, 1):
+        pl.when(jobs[side][1])(jobs[side][0].start)
     return jobs
+
+
+def unpack(value):
+    lane = lax.broadcasted_iota(jnp.int32, (value.shape[0], LANES), 1)
+    keep = (lane < C).astype(F32).astype(BF16)
+    return value[:, 0:LANES] * keep, pltpu.roll(value[:, 128:384], 192, 1) * keep
+
+
+def place_rim(field, rows_in, cols_in, view_row):
+    for j in range(2):
+        if view_row != 1:
+            pair = unpack(rows_in[view_row // 2, j].reshape(T * V, 384))
+            for k in range(2):
+                field[view_row, 1 + 2 * j + k, 1 : 1 + T] = pair[k].reshape(T, V, LANES)
+        for side, at in ((0, 0), (1, T + 1)):
+            pair = unpack(cols_in[view_row, side, j])
+            for k in range(2):
+                field[view_row, 1 + 2 * j + k, at] = pair[k]
 
 
 def greet():
@@ -252,26 +279,41 @@
 
 
 def step_kernel(
-    x_ref, cot_ref, w_ref, gi_ref, gk_ref,
-    xp, gp, xc, wv, wt, acc, gall, dw, pair,
+    x_hbm, cot_hbm, w_ref, gi_ref, gk_ref,
+    x_ref, cot_ref, gi_out, packed, edges, rows_in, cols_in, xp, gp, xc, wv, wt, acc, gall, dw, pair,
     first_a, first_b, first_c, got_a, got_b, got_c, sum_a, sum_b, sum_c,
     next_b, near_a, near_b, near_c, last_a, last_b, last_c, ends, both, left, right,
-    halo_send, halo_recv, wsem, pair_sems, first_send, first_recv, next_sems, last_sems, core_sems,
+    halo_send, halo_recv, in_sems, wsem, pair_sems, first_send, first_recv, next_sems, last_sems, core_sems,
 ):
     chip_x, chip_y, chip_z, core = place()
+    xcopy = pltpu.make_async_copy(x_hbm, x_ref, in_sems.at[0])
+    ccopy = pltpu.make_async_copy(cot_hbm, cot_ref, in_sems.at[1])
     wcopy = pltpu.make_async_copy(w_ref, wv.at[pl.ds(0, ROWS)], wsem)
+    xcopy.start()
     wcopy.start()
+    ccopy.start()
+    rows_in[...] = jnp.zeros_like(rows_in)
+    cols_in[...] = jnp.zeros_like(cols_in)
+    peers = greet()
     xp[...] = jnp.zeros_like(xp)
-    peers = greet()
-    for s in range(S):
-        block = jnp.swapaxes(x_ref[0, :, s].astype(F32), 0, 1).astype(BF16)
-        xp[1, 1 + s, 1 : 1 + T, :, 0:C] = block
     gp[...] = jnp.zeros_like(gp)
     rest = pl.ds(ROWS, WIDE - GROUP)
     wv[rest, :] = jnp.zeros((WIDE - GROUP, C), BF16)
     wt[rest, :] = jnp.zeros((WIDE - GROUP, C), BF16)
+    xcopy.wait()
+    for s in range(S):
+        block = jnp.swapaxes(x_ref[0, :, s].astype(F32), 0, 1).astype(BF16)
+        xp[1, 1 + s, 1 : 1 + T, :, 0:C] = block
+
+    def halo(field, k):
+        pads = (packed.at[k], edges.at[k], rows_in.at[k], cols_in.at[k])
+        return start_halo(field, *pads, halo_send.at[k], halo_recv.at[k])
+
+    def rim(field, k, view_row):
+        place_rim(field, rows_in.at[k], cols_in.at[k], view_row)
+
     pl.semaphore_wait(pltpu.get_barrier_semaphore(), peers)
-    jobs = start_halo(xp, halo_send.at[0], halo_recv.at[0])
+    jobs = halo(xp, 0)
 
     wcopy.wait()
 
@@ -283,16 +325,19 @@
 
     for copy, _, got in jobs[:2]:
         pl.when(got)(copy.wait_recv)
+    rim(xp, 0, 1)
     unfold(xp, xc.at[1], 1)
     correlate(xc.at[1], wv, acc, 1, True)
     for copy, _, got in jobs[2:]:
         pl.when(got)(copy.wait_recv)
     for view_row in (0, 2):
+        rim(xp, 0, view_row)
         unfold(xp, xc.at[view_row], view_row)
         correlate(xc.at[view_row], wv, acc, view_row, False)
     for copy, sent, _ in jobs:
         pl.when(sent)(copy.wait_send)
 
+    ccopy.wait()
     preact = shifted(acc[0], 1) + acc[1] + shifted(acc[2], -1)
     for s in range(S):
         upstream = jnp.swapaxes(cot_ref[0, :, s].astype(F32), 0, 1).reshape(T * V, C)
@@ -300,7 +345,7 @@
         sigmoid = jax.nn.sigmoid(pre)
         grad = upstream * sigmoid * (1.0 + pre * (1.0 - sigmoid))
         gp[1, 1 + s, 1 : 1 + T, :, 0:C] = grad.astype(BF16).reshape(T, V, C)
-    jobs = start_halo(gp, halo_send.at[1], halo_recv.at[1])
+    jobs = halo(gp, 1)
     grad = gp[1, 1 : 1 + S, 1 : 1 + T].reshape(CELLS, LANES)
     wide = grad.astype(F32)
     gall[:, 0:256] = shifted(wide, -1).astype(BF16)
@@ -338,6 +383,7 @@
         scatters[2].start(a)
 
     def input_terms(view_row, first):
+        rim(gp, 1, view_row)
         unfold(gp, xc.at[view_row], view_row)
         correlate(xc.at[view_row], wt, acc, view_row, first)
 
@@ -388,7 +434,9 @@
     total = shifted(acc[0], 1) + acc[1] + shifted(acc[2], -1)
     for s in range(S):
         block = total[s * T * V : (s + 1) * T * V].reshape(T, V, C)
-        gi_ref[0, :, s] = jnp.swapaxes(block, 0, 1).astype(BF16)
+        gi_out[0, :, s] = jnp.swapaxes(block, 0, 1).astype(BF16)
+    gcopy = pltpu.make_async_copy(gi_out, gi_ref, in_sems.at[2])
+    gcopy.start()
 
     for copy in sends:
         copy.wait_recv()
@@ -425,6 +473,7 @@
         for k in range(3):
             value += ends[3 * plane + k].astype(F32)
         both[core, plane] = value
+    gcopy.wait()
     send_to(sibling(), both.at[core], both.at[core], core_sems, 0).wait()
 
     for k in range(2):
@@ -457,9 +506,14 @@
             jax.ShapeDtypeStruct(inputs.shape, BF16),
             jax.ShapeDtypeStruct((480, 128), F32),
         ),
-        in_specs=[vmem, vmem, anywhere],
-        out_specs=(vmem, vmem),
+        in_specs=[anywhere, anywhere, anywhere],
+        out_specs=(anywhere, vmem),
         scratch_shapes=[
+            *(pltpu.VMEM(inputs.shape, BF16) for _ in range(3)),
+            pltpu.VMEM((2, 2, T, V, 384), BF16),
+            pltpu.VMEM((2, 2, 2, V, 384), BF16),
+            pltpu.VMEM((2, 2, 2, T, V, 384), BF16),
+            pltpu.VMEM((2, 3, 2, 2, V, 384), BF16),
             pltpu.VMEM(padded, BF16),
             pltpu.VMEM(padded, BF16),
             pltpu.VMEM((3, CELLS, WIDE), BF16),
@@ -487,6 +541,7 @@
             pltpu.VMEM((320, 128), F32),
             dma(2, 8),
             dma(2, 8),
+            dma(3),
             pltpu.SemaphoreType.DMA,
             dma(2, 3),
             dma(3, 4, 3),

time: 65.1 us -> 64 us (0.983)
  Pallas kernels: 60.8 us -> 59.7 us
    pallas_call x1, Pallas kernels: 60.8 us -> 59.7 us  [local(): pl.pallas_call(step_kernel, out_shape=(jax.ShapeDtypeStruct(inputs.shape,...]
where the time goes in v4:
time: 64 us; the launch traced here: 63.8 us
  Pallas kernels  59.7 us (93%)
  other arithmetic  1.73 us (3%)
  local copies, waits for them, and re-layouts  1.68 us (3%)
  between operations  0.72 us (1%)
    pallas_call x1, Pallas kernels, local(): pl.pallas_call(step_kernel, out_shape=(jax.ShapeDtypeStruct(inputs.shape,...  59.7 us
    div x1, other arithmetic, local(): moment_next / first_fix / (jnp.sqrt(square_next / second_fix) + epsilon)  1.73 us
    unnamed x5, local copies, waits for them, and re-layouts  1.68 us

profile of v4, /device:TPU:1, one launch (start us, length us, event | category | flops | bytes accessed | tf_op | source)
XLA Modules:
  0.0 63.8 jit_solution(3530895281811737847)
XLA Ops:
  0.7 0.0 copy-start
  0.7 0.0 copy-start.1
  0.7 59.7 %shard_map.84 = (bf16[1,16,4,8,192]{4,3,2,1,0:T(8,128)(2,1)}, f32[480,128]{1,0:T(8,128)}) custom-call(bf16[1,16,4,8,192]{4,3,2,1,0:T(8,128)(2,1)} %x_hbm.1, bf16[1,16,4,8,192]{4,3,2,1,0:T(8,128)(2,1)} %cot_hbm.1, bf16[15552,192]{1,0:T(8,128)(2,1)} %bitcast.3), custom_call_target="tpu_custom_call" | custom-call | flops 8999999488 | bytes 10000000 | tf_op jit(solution)/shard_map/pallas_call | solution.py:503
  60.4 0.0 copy-done
  60.4 0.0 copy-done.1
  60.4 1.7 %add_divide_fusion = (f32[23328]{0:T(1024)}, f32[23328]{0:T(1024)}, f32[23328]{0:T(1024)}) fusion(f32[61440]{0:T(1024)} %bitcast.2, s32[]{:T(128)S(6)} %select_n.13, f32[23328]{0:T(1024)S(1)} %copy-done, f32[23328]{0:T(1024)S(1)} %copy-done.1), kind=kLoop, calls=%fused_computation | loop fusion | flops 279936 | bytes 559876 | tf_op jit(solution)/shard_map/div | solution.py:568
  62.2 1.7 %copy.10 = bf16[1,16,4,8,192]{4,3,2,1,0:T(8,128)(2,1)} copy(bf16[1,16,4,8,192]{4,3,2,1,0:T(8,128)(2,1)} %get-tuple-element.15) | data formatting | bytes 393216
Async XLA Ops:
  0.7 59.7 %copy-start = (f32[23328]{0:T(1024)S(1)}, f32[23328]{0:T(1024)}, u32[]{:S(2)}) copy-start(f32[23328]{0:T(1024)} %param.9) | copy-start | bytes 279940
  0.7 59.7 %copy-start.1 = (f32[23328]{0:T(1024)S(1)}, f32[23328]{0:T(1024)}, u32[]{:S(2)}) copy-start(f32[23328]{0:T(1024)} %param.8) | copy-start | bytes 279940

commit v5 on v4

--- a/solution.py
+++ b/solution.py
@@ -157,7 +157,9 @@
 
 UNITS = 243
 TILE = (16, 128)
-LENGTHS = (64, 72, 80)
+SHARE = 243 * C // 2
+BAND = 17
+LENGTHS = (64, 4 * BAND, 80)
 
 
 def window(chips, index, count):
@@ -212,7 +214,7 @@
                     found.append((x, low - start, low, high - low))
         return found
     if plane == 1:
-        return [(p % 4, 18 * (p // 4), window(4, p, 18), 18) for p in range(16)]
+        return [(p % 4, BAND * (p // 4), window(4, p, BAND), BAND) for p in range(16)]
     return [(q % 4, 5 * (q // 4), window(1, q, 5), 5) for q in range(64)]
 
 
@@ -282,7 +284,7 @@
     x_hbm, cot_hbm, w_ref, gi_ref, gk_ref,
     x_ref, cot_ref, gi_out, packed, edges, rows_in, cols_in, xp, gp, xc, wv, wt, acc, gall, dw, pair,
     first_a, first_b, first_c, got_a, got_b, got_c, sum_a, sum_b, sum_c,
-    next_b, near_a, near_b, near_c, last_a, last_b, last_c, ends, both, left, right,
+    next_b, near_a, near_b, near_c, last_a, last_b, last_c, ends, both, left, right, flat,
     halo_send, halo_recv, in_sems, wsem, pair_sems, first_send, first_recv, next_sems, last_sems, core_sems,
 ):
     chip_x, chip_y, chip_z, core = place()
@@ -312,17 +314,19 @@
     def rim(field, k, view_row):
         place_rim(field, rows_in.at[k], cols_in.at[k], view_row)
 
+    wcopy.wait()
+
+    def turn(low, high):
+        @pl.loop(low, high)
+        def _(tap):
+            src = pl.ds(pl.multiple_of((80 - tap) * C, 64), C)
+            dst = pl.ds(pl.multiple_of(tap * C, 64), C)
+            wt[dst, :] = wv[src, :].T
+
+    turn(0, 45)
     pl.semaphore_wait(pltpu.get_barrier_semaphore(), peers)
     jobs = halo(xp, 0)
-
-    wcopy.wait()
-
-    @pl.loop(0, 81)
-    def _(tap):
-        src = pl.ds(pl.multiple_of((80 - tap) * C, 64), C)
-        dst = pl.ds(pl.multiple_of(tap * C, 64), C)
-        wt[dst, :] = wv[src, :].T
-
+    turn(45, 81)
     for copy, _, got in jobs[:2]:
         pl.when(got)(copy.wait_recv)
     rim(xp, 0, 1)
@@ -405,7 +409,7 @@
         ring.wait()
     sum_a[...] = scatters[0].total(pl.ds(0, 64))
     for x in range(4):
-        sum_b[x] = scatters[1].total(pl.ds(18 * x, 18))
+        sum_b[x] = scatters[1].total(pl.ds(BAND * x, BAND))
 
     @pl.loop(0, 16)
     def _(p):
@@ -416,12 +420,12 @@
 
     def next_part(plane, to):
         if plane == 0:
-            return sum_a.at[pl.ds(window(4, chip_x * 4 + to, 18) - window(16, chip_x, 64), 18)]
+            return sum_a.at[pl.ds(window(4, chip_x * 4 + to, BAND) - window(16, chip_x, 64), BAND)]
         return (next_b if plane == 1 else sum_c).at[to]
 
     for x in range(4):
         for z in range(4):
-            start = window(1, x * 16 + chip_y * 4 + z, 5) - window(4, x * 4 + chip_y, 18)
+            start = window(1, x * 16 + chip_y * 4 + z, 5) - window(4, x * 4 + chip_y, BAND)
             next_b[z, x] = sum_b[x, pl.ds(start, 5)]
     sends = []
     for step in (2, 1, 3):
@@ -453,7 +457,7 @@
 
     def last_part(plane, to):
         if plane == 0:
-            return last_a.at[pl.ds(window(1, column * 4 + to, 5) - window(4, column, 18), 5)]
+            return last_a.at[pl.ds(window(1, column * 4 + to, 5) - window(4, column, BAND), 5)]
         return (last_b if plane == 1 else last_c).at[to]
 
     lasts = []
@@ -487,10 +491,18 @@
     count = 160
     odd = pltpu.roll(left[pl.ds(1, count, stride=2), :], 64, 1)
     head = lax.broadcasted_iota(jnp.int32, (count, 128), 1) < 64
-    gk_ref[pl.ds(0, count, stride=3), :] = left[pl.ds(0, count, stride=2), :]
-    gk_ref[pl.ds(1, count, stride=3), :] = jnp.where(head, right[pl.ds(0, count, stride=2), :], odd)
+    flat[pl.ds(0, count, stride=3), :] = left[pl.ds(0, count, stride=2), :]
+    flat[pl.ds(1, count, stride=3), :] = jnp.where(head, right[pl.ds(0, count, stride=2), :], odd)
     rest = pltpu.roll(right[pl.ds(1, count, stride=2), :], 64, 1)
-    gk_ref[pl.ds(2, count, stride=3), :] = jnp.where(head, odd, rest)
+    flat[pl.ds(2, count, stride=3), :] = jnp.where(head, odd, rest)
+    flat[480:488] = jnp.zeros((8, 128), F32)
+    begin = (column * 4 + chip_z) * (243 * C) + core * SHARE - window(1, column * 4 + chip_z, 5) * (64 * C)
+    row, turn_by = begin // 128, begin % 128
+    held = gk_ref.shape[0]
+    before = lax.broadcasted_iota(jnp.int32, (held, 128), 1) < 128 - turn_by
+    this = pltpu.roll(flat[pl.ds(row, held), :], (128 - turn_by) % 128, 1)
+    after = pltpu.roll(flat[pl.ds(row + 1, held), :], (128 - turn_by) % 128, 1)
+    gk_ref[...] = jnp.where(before, this, after)
 
 
 def local(inputs, cotangent, kernel, moment_one, moment_two):
@@ -500,11 +512,11 @@
     tiles = lambda *lead: pltpu.VMEM((*lead, *TILE), BF16)
     dma = lambda *shape: pltpu.SemaphoreType.DMA(shape)
     long_kernel = pltpu.VMEM((ROWS + WIDE - GROUP, C), BF16)
-    grad_input, window_grad = pl.pallas_call(
+    grad_input, share_grad = pl.pallas_call(
         step_kernel,
         out_shape=(
             jax.ShapeDtypeStruct(inputs.shape, BF16),
-            jax.ShapeDtypeStruct((480, 128), F32),
+            jax.ShapeDtypeStruct((184, 128), F32),
         ),
         in_specs=[anywhere, anywhere, anywhere],
         out_specs=(anywhere, vmem),
@@ -526,19 +538,20 @@
             *(tiles(4, n) for n in LENGTHS),
             *(tiles(3, n) for n in LENGTHS),
             tiles(64),
-            tiles(4, 18),
+            tiles(4, BAND),
             tiles(4, 4, 5),
             tiles(4, 4, 5),
-            tiles(3, 18),
+            tiles(3, BAND),
             tiles(3, 4, 5),
             tiles(3, 4, 5),
-            tiles(18),
+            tiles(BAND),
             tiles(4, 5),
             tiles(4, 5),
             tiles(9, 5),
             pltpu.VMEM((2, 3, 5, *TILE), F32),
             pltpu.VMEM((320, 128), F32),
             pltpu.VMEM((320, 128), F32),
+            pltpu.VMEM((488, 128), F32),
             dma(2, 8),
             dma(2, 8),
             dma(3),
@@ -556,9 +569,7 @@
         cost_estimate=pl.CostEstimate(flops=9 * 10**9, bytes_accessed=10**7, transcendentals=10**5),
     )(inputs, cotangent, kernel.reshape(ROWS, C))
     share_len = moment_one.shape[0]
-    chip = lax.axis_index("ang") * 4 + lax.axis_index("sp") // 2
-    begin = lax.axis_index(("ang", "sp")) * share_len - window(1, chip, 5) * (64 * C)
-    share = lax.dynamic_slice_in_dim(window_grad.reshape(-1), begin, share_len, 0)
+    share = share_grad.reshape(-1)[:share_len]
     pixels = CELLS * lax.axis_size("ang") * lax.axis_size("sp")
     grad_share = share * F32(1.0 / math.sqrt(pixels))
     moment_next = beta_one * moment_one + (1.0 - beta_one) * grad_share

time: 64 us -> 65.7 us (1.027)
  Pallas kernels: 59.7 us -> 61.5 us
    pallas_call x1, Pallas kernels: 59.7 us -> 61.5 us  [local(): pl.pallas_call(step_kernel, out_shape=(jax.ShapeDtypeStruct(inputs.shape,...]
where the time goes in v5:
time: 65.7 us; the launch traced here: 65.5 us
  Pallas kernels  61.5 us (94%)
  local copies, waits for them, and re-layouts  1.68 us (3%)
  other arithmetic  1.62 us (2%)
  between operations  0.67 us (1%)
    pallas_call x1, Pallas kernels, local(): pl.pallas_call(step_kernel, out_shape=(jax.ShapeDtypeStruct(inputs.shape,...  61.5 us
    unnamed x5, local copies, waits for them, and re-layouts  1.68 us
    div x1, other arithmetic, local(): moment_next / first_fix / (jnp.sqrt(square_next / second_fix) + epsilon)  1.62 us

profile of v5, /device:TPU:1, one launch (start us, length us, event | category | flops | bytes accessed | tf_op | source)
XLA Modules:
  0.0 65.5 jit_solution(14885680186305499524)
XLA Ops:
  0.6 0.0 copy-start
  0.6 0.0 copy-start.1
  0.7 61.5 %shard_map.84 = (bf16[1,16,4,8,192]{4,3,2,1,0:T(8,128)(2,1)}, f32[184,128]{1,0:T(8,128)}) custom-call(bf16[1,16,4,8,192]{4,3,2,1,0:T(8,128)(2,1)} %x_hbm.1, bf16[1,16,4,8,192]{4,3,2,1,0:T(8,128)(2,1)} %cot_hbm.1, bf16[15552,192]{1,0:T(8,128)(2,1)} %bitcast.3), custom_call_target="tpu_custom_call" | custom-call | flops 8999999488 | bytes 10000000 | tf_op jit(solution)/shard_map/pallas_call | solution.py:515
  62.2 0.0 copy-done
  62.2 0.0 copy-done.1
  62.2 1.6 %add_divide_fusion = (f32[23328]{0:T(1024)}, f32[23328]{0:T(1024)}, f32[23328]{0:T(1024)}) fusion(f32[23552]{0:T(1024)} %bitcast.2, f32[23328]{0:T(1024)S(1)} %copy-done, f32[23328]{0:T(1024)S(1)} %copy-done.1), kind=kLoop, calls=%fused_computation | loop fusion | flops 279936 | bytes 559872 | tf_op jit(solution)/shard_map/div | solution.py:579
  63.8 1.7 %copy.10 = bf16[1,16,4,8,192]{4,3,2,1,0:T(8,128)(2,1)} copy(bf16[1,16,4,8,192]{4,3,2,1,0:T(8,128)(2,1)} %get-tuple-element.15) | data formatting | bytes 393216
Async XLA Ops:
  0.6 61.6 %copy-start = (f32[23328]{0:T(1024)S(1)}, f32[23328]{0:T(1024)}, u32[]{:S(2)}) copy-start(f32[23328]{0:T(1024)} %param.9) | copy-start | bytes 279940
  0.6 61.6 %copy-start.1 = (f32[23328]{0:T(1024)S(1)}, f32[23328]{0:T(1024)}, u32[]{:S(2)}) copy-start(f32[23328]{0:T(1024)} %param.8) | copy-start | bytes 279940

commit v6 on v5

--- a/solution.py
+++ b/solution.py
@@ -314,6 +314,8 @@
     def rim(field, k, view_row):
         place_rim(field, rows_in.at[k], cols_in.at[k], view_row)
 
+    pl.semaphore_wait(pltpu.get_barrier_semaphore(), peers)
+    jobs = halo(xp, 0)
     wcopy.wait()
 
     def turn(low, high):
@@ -323,15 +325,13 @@
             dst = pl.ds(pl.multiple_of(tap * C, 64), C)
             wt[dst, :] = wv[src, :].T
 
-    turn(0, 45)
-    pl.semaphore_wait(pltpu.get_barrier_semaphore(), peers)
-    jobs = halo(xp, 0)
-    turn(45, 81)
+    turn(0, 40)
     for copy, _, got in jobs[:2]:
         pl.when(got)(copy.wait_recv)
     rim(xp, 0, 1)
     unfold(xp, xc.at[1], 1)
     correlate(xc.at[1], wv, acc, 1, True)
+    turn(40, 60)
     for copy, _, got in jobs[2:]:
         pl.when(got)(copy.wait_recv)
     for view_row in (0, 2):
@@ -397,6 +397,7 @@
         kernel_terms(xc, gall, dw, a)
         pairs.append(exchange(a))
         scatter(pairs[a - 1], a - 1)
+    turn(60, 81)
     for copy, _, got in jobs[:2]:
         pl.when(got)(copy.wait_recv)
     input_terms(1, True)

time: 65.7 us -> 64.8 us (0.986)
  Pallas kernels: 61.5 us -> 60.1 us
    pallas_call x1, Pallas kernels: 61.5 us -> 60.1 us  [local(): pl.pallas_call(step_kernel, out_shape=(jax.ShapeDtypeStruct(inputs.shape,...]
where the time goes in v6:
time: 64.8 us; the launch traced here: 64.1 us
  Pallas kernels  60.1 us (93%)
  local copies, waits for them, and re-layouts  1.68 us (3%)
  other arithmetic  1.62 us (2%)
  between operations  0.67 us (1%)
    pallas_call x1, Pallas kernels, local(): pl.pallas_call(step_kernel, out_shape=(jax.ShapeDtypeStruct(inputs.shape,...  60.1 us
    unnamed x5, local copies, waits for them, and re-layouts  1.68 us
    div x1, other arithmetic, local(): moment_next / first_fix / (jnp.sqrt(square_next / second_fix) + epsilon)  1.62 us

profile of v6, /device:TPU:1, one launch (start us, length us, event | category | flops | bytes accessed | tf_op | source)
XLA Modules:
  0.0 64.1 jit_solution(4523095733480421236)
XLA Ops:
  0.6 0.0 copy-start
  0.6 0.0 copy-start.1
  0.7 60.1 %shard_map.84 = (bf16[1,16,4,8,192]{4,3,2,1,0:T(8,128)(2,1)}, f32[184,128]{1,0:T(8,128)}) custom-call(bf16[1,16,4,8,192]{4,3,2,1,0:T(8,128)(2,1)} %x_hbm.1, bf16[1,16,4,8,192]{4,3,2,1,0:T(8,128)(2,1)} %cot_hbm.1, bf16[15552,192]{1,0:T(8,128)(2,1)} %bitcast.3), custom_call_target="tpu_custom_call" | custom-call | flops 8999999488 | bytes 10000000 | tf_op jit(solution)/shard_map/pallas_call | solution.py:516
  60.8 0.0 copy-done
  60.8 0.0 copy-done.1
  60.8 1.6 %add_divide_fusion = (f32[23328]{0:T(1024)}, f32[23328]{0:T(1024)}, f32[23328]{0:T(1024)}) fusion(f32[23552]{0:T(1024)} %bitcast.2, f32[23328]{0:T(1024)S(1)} %copy-done, f32[23328]{0:T(1024)S(1)} %copy-done.1), kind=kLoop, calls=%fused_computation | loop fusion | flops 279936 | bytes 559872 | tf_op jit(solution)/shard_map/div | solution.py:580
  62.4 1.7 %copy.10 = bf16[1,16,4,8,192]{4,3,2,1,0:T(8,128)(2,1)} copy(bf16[1,16,4,8,192]{4,3,2,1,0:T(8,128)(2,1)} %get-tuple-element.15) | data formatting | bytes 393216
Async XLA Ops:
  0.6 60.1 %copy-start = (f32[23328]{0:T(1024)S(1)}, f32[23328]{0:T(1024)}, u32[]{:S(2)}) copy-start(f32[23328]{0:T(1024)} %param.9) | copy-start | bytes 279940
  0.6 60.1 %copy-start.1 = (f32[23328]{0:T(1024)S(1)}, f32[23328]{0:T(1024)}, u32[]{:S(2)}) copy-start(f32[23328]{0:T(1024)} %param.8) | copy-start | bytes 279940

commit v7 on v6

--- a/solution.py
+++ b/solution.py
@@ -157,7 +157,6 @@
 
 UNITS = 243
 TILE = (16, 128)
-SHARE = 243 * C // 2
 BAND = 17
 LENGTHS = (64, 4 * BAND, 80)
 
@@ -284,7 +283,7 @@
     x_hbm, cot_hbm, w_ref, gi_ref, gk_ref,
     x_ref, cot_ref, gi_out, packed, edges, rows_in, cols_in, xp, gp, xc, wv, wt, acc, gall, dw, pair,
     first_a, first_b, first_c, got_a, got_b, got_c, sum_a, sum_b, sum_c,
-    next_b, near_a, near_b, near_c, last_a, last_b, last_c, ends, both, left, right, flat,
+    next_b, near_a, near_b, near_c, last_a, last_b, last_c, ends, both, left, right,
     halo_send, halo_recv, in_sems, wsem, pair_sems, first_send, first_recv, next_sems, last_sems, core_sems,
 ):
     chip_x, chip_y, chip_z, core = place()
@@ -372,19 +371,19 @@
 
     def scatter(copy, a):
         copy.wait_recv()
-        for plane in range(2):
+        chips = [q for q, (_, _, start, count) in enumerate(pieces(2)) if ready(start, count) == a]
+
+        @pl.loop(chips[0], chips[-1] + 1)
+        def _(q):
+            at = pl.ds((q // 4) * 5, 5)
+            first_c[q % 4, at] = both_cores(2, window(1, q, 5), 5)
+
+        scatters[2].start(a)
+        for plane in (1, 0):
             for target, at, start, count in pieces(plane):
                 if ready(start, count) == a:
                     firsts[plane][target, at : at + count] = both_cores(plane, start, count)
             scatters[plane].start(a)
-        chips = [q for q, (_, _, start, count) in enumerate(pieces(2)) if ready(start, count) == a]
-
-        @pl.loop(chips[0], chips[-1] + 1)
-        def _(q):
-            at = pl.ds((q // 4) * 5, 5)
-            first_c[q % 4, at] = both_cores(2, window(1, q, 5), 5)
-
-        scatters[2].start(a)
 
     def input_terms(view_row, first):
         rim(gp, 1, view_row)
@@ -406,16 +405,6 @@
         pl.when(got)(copy.wait_recv)
     input_terms(0, False)
 
-    for ring in scatters:
-        ring.wait()
-    sum_a[...] = scatters[0].total(pl.ds(0, 64))
-    for x in range(4):
-        sum_b[x] = scatters[1].total(pl.ds(BAND * x, BAND))
-
-    @pl.loop(0, 16)
-    def _(p):
-        sum_c[p // 4, p % 4] = scatters[2].total(pl.ds(5 * p, 5))
-
     chips = (chip_x, chip_y, chip_z)
     column = chip_x * 4 + chip_y
 
@@ -424,16 +413,38 @@
             return sum_a.at[pl.ds(window(4, chip_x * 4 + to, BAND) - window(16, chip_x, 64), BAND)]
         return (next_b if plane == 1 else sum_c).at[to]
 
-    for x in range(4):
-        for z in range(4):
-            start = window(1, x * 16 + chip_y * 4 + z, 5) - window(4, x * 4 + chip_y, BAND)
-            next_b[z, x] = sum_b[x, pl.ds(start, 5)]
-    sends = []
-    for step in (2, 1, 3):
-        for plane, axis in enumerate((1, 2, 0)):
+    def last_part(plane, to):
+        if plane == 0:
+            return last_a.at[pl.ds(window(1, column * 4 + to, 5) - window(4, column, BAND), 5)]
+        return (last_b if plane == 1 else last_c).at[to]
+
+    nears = (near_a, near_b, near_c)
+    second, third = (1, 2, 0), (2, 0, 1)
+    sends = {}
+    for plane in range(3):
+        scatters[plane].wait()
+        if plane == 0:
+            sum_a[...] = scatters[0].total(pl.ds(0, 64))
+        elif plane == 1:
+            for x in range(4):
+                sum_b[x] = scatters[1].total(pl.ds(BAND * x, BAND))
+            for x in range(4):
+                for z in range(4):
+                    start = window(1, x * 16 + chip_y * 4 + z, 5) - window(4, x * 4 + chip_y, BAND)
+                    next_b[z, x] = sum_b[x, pl.ds(start, 5)]
+        else:
+
+            @pl.loop(0, 16)
+            def _(p):
+                sum_c[p // 4, p % 4] = scatters[2].total(pl.ds(5 * p, 5))
+
+        axis = second[plane]
+        for step in (2, 1, 3):
             src = next_part(plane, lax.rem(chips[axis] + step, 4))
-            dst = (near_a, near_b, near_c)[plane].at[step - 1]
-            sends.append(send_to(peer_along(axis, step), src, dst, next_sems.at[plane], step - 1))
+            dst = nears[plane].at[step - 1]
+            sends[plane, step] = send_to(
+                peer_along(axis, step), src, dst, next_sems.at[plane], step - 1
+            )
 
     input_terms(2, False)
     total = shifted(acc[0], 1) + acc[1] + shifted(acc[2], -1)
@@ -443,42 +454,33 @@
     gcopy = pltpu.make_async_copy(gi_out, gi_ref, in_sems.at[2])
     gcopy.start()
 
-    for copy in sends:
-        copy.wait_recv()
-
-    def near_total(plane, near):
-        value = next_part(plane, chips[(1, 2, 0)[plane]])[...].astype(F32)
+    lasts = {}
+    for plane in range(3):
+        for step in (1, 3, 2):
+            sends[plane, step].wait_recv()
+        value = next_part(plane, chips[second[plane]])[...].astype(F32)
         for k in range(3):
-            value += near[k].astype(F32)
-        return value.astype(BF16)
-
-    last_a[...] = near_total(0, near_a)
-    last_b[...] = near_total(1, near_b)
-    last_c[...] = near_total(2, near_c)
-
-    def last_part(plane, to):
-        if plane == 0:
-            return last_a.at[pl.ds(window(1, column * 4 + to, 5) - window(4, column, BAND), 5)]
-        return (last_b if plane == 1 else last_c).at[to]
-
-    lasts = []
-    for step in (2, 1, 3):
-        for plane, axis in enumerate((2, 0, 1)):
+            value += nears[plane][k].astype(F32)
+        (last_a, last_b, last_c)[plane][...] = value.astype(BF16)
+        axis = third[plane]
+        for step in (2, 1, 3):
             src = last_part(plane, lax.rem(chips[axis] + step, 4))
             slot = 3 * plane + step - 1
-            lasts.append(send_to(peer_along(axis, step), src, ends.at[slot], last_sems, slot))
+            lasts[plane, step] = send_to(
+                peer_along(axis, step), src, ends.at[slot], last_sems, slot
+            )
     for copy, sent, _ in jobs:
         pl.when(sent)(copy.wait_send)
-    for copy in (*pairs, *sends):
+    for copy in (*pairs, *sends.values()):
         copy.wait_send()
-    for copy in lasts:
-        copy.wait()
-    for plane, axis in enumerate((2, 0, 1)):
-        value = last_part(plane, chips[axis])[...].astype(F32)
+    gcopy.wait()
+    for plane in range(3):
+        for step in (1, 3, 2):
+            lasts[plane, step].wait()
+        value = last_part(plane, chips[third[plane]])[...].astype(F32)
         for k in range(3):
             value += ends[3 * plane + k].astype(F32)
         both[core, plane] = value
-    gcopy.wait()
     send_to(sibling(), both.at[core], both.at[core], core_sems, 0).wait()
 
     for k in range(2):
@@ -492,18 +494,10 @@
     count = 160
     odd = pltpu.roll(left[pl.ds(1, count, stride=2), :], 64, 1)
     head = lax.broadcasted_iota(jnp.int32, (count, 128), 1) < 64
-    flat[pl.ds(0, count, stride=3), :] = left[pl.ds(0, count, stride=2), :]
-    flat[pl.ds(1, count, stride=3), :] = jnp.where(head, right[pl.ds(0, count, stride=2), :], odd)
+    gk_ref[pl.ds(0, count, stride=3), :] = left[pl.ds(0, count, stride=2), :]
+    gk_ref[pl.ds(1, count, stride=3), :] = jnp.where(head, right[pl.ds(0, count, stride=2), :], odd)
     rest = pltpu.roll(right[pl.ds(1, count, stride=2), :], 64, 1)
-    flat[pl.ds(2, count, stride=3), :] = jnp.where(head, odd, rest)
-    flat[480:488] = jnp.zeros((8, 128), F32)
-    begin = (column * 4 + chip_z) * (243 * C) + core * SHARE - window(1, column * 4 + chip_z, 5) * (64 * C)
-    row, turn_by = begin // 128, begin % 128
-    held = gk_ref.shape[0]
-    before = lax.broadcasted_iota(jnp.int32, (held, 128), 1) < 128 - turn_by
-    this = pltpu.roll(flat[pl.ds(row, held), :], (128 - turn_by) % 128, 1)
-    after = pltpu.roll(flat[pl.ds(row + 1, held), :], (128 - turn_by) % 128, 1)
-    gk_ref[...] = jnp.where(before, this, after)
+    gk_ref[pl.ds(2, count, stride=3), :] = jnp.where(head, odd, rest)
 
 
 def local(inputs, cotangent, kernel, moment_one, moment_two):
@@ -513,11 +507,11 @@
     tiles = lambda *lead: pltpu.VMEM((*lead, *TILE), BF16)
     dma = lambda *shape: pltpu.SemaphoreType.DMA(shape)
     long_kernel = pltpu.VMEM((ROWS + WIDE - GROUP, C), BF16)
-    grad_input, share_grad = pl.pallas_call(
+    grad_input, window_grad = pl.pallas_call(
         step_kernel,
         out_shape=(
             jax.ShapeDtypeStruct(inputs.shape, BF16),
-            jax.ShapeDtypeStruct((184, 128), F32),
+            jax.ShapeDtypeStruct((480, 128), F32),
         ),
         in_specs=[anywhere, anywhere, anywhere],
         out_specs=(anywhere, vmem),
@@ -552,7 +546,6 @@
             pltpu.VMEM((2, 3, 5, *TILE), F32),
             pltpu.VMEM((320, 128), F32),
             pltpu.VMEM((320, 128), F32),
-            pltpu.VMEM((488, 128), F32),
             dma(2, 8),
             dma(2, 8),
             dma(3),
@@ -570,7 +563,9 @@
         cost_estimate=pl.CostEstimate(flops=9 * 10**9, bytes_accessed=10**7, transcendentals=10**5),
     )(inputs, cotangent, kernel.reshape(ROWS, C))
     share_len = moment_one.shape[0]
-    share = share_grad.reshape(-1)[:share_len]
+    chip = lax.axis_index("ang") * 4 + lax.axis_index("sp") // 2
+    begin = lax.axis_index(("ang", "sp")) * share_len - window(1, chip, 5) * (64 * C)
+    share = lax.dynamic_slice_in_dim(window_grad.reshape(-1), begin, share_len, 0)
     pixels = CELLS * lax.axis_size("ang") * lax.axis_size("sp")
     grad_share = share * F32(1.0 / math.sqrt(pixels))
     moment_next = beta_one * moment_one + (1.0 - beta_one) * grad_share

time: 64.8 us -> 65.2 us (level)
  Pallas kernels: 60.1 us -> 60.9 us
    pallas_call x1, Pallas kernels: 60.1 us -> 60.9 us  [local(): pl.pallas_call(step_kernel, out_shape=(jax.ShapeDtypeStruct(inputs.shape,...]
where the time goes in v7:
time: 65.2 us; the launch traced here: 65 us
  Pallas kernels  60.9 us (93%)
  other arithmetic  1.73 us (3%)
  local copies, waits for them, and re-layouts  1.68 us (3%)
  between operations  0.72 us (1%)
    pallas_call x1, Pallas kernels, local(): pl.pallas_call(step_kernel, out_shape=(jax.ShapeDtypeStruct(inputs.shape,...  60.9 us
    div x1, other arithmetic, local(): moment_next / first_fix / (jnp.sqrt(square_next / second_fix) + epsilon)  1.73 us
    unnamed x5, local copies, waits for them, and re-layouts  1.68 us

profile of v7, /device:TPU:1, one launch (start us, length us, event | category | flops | bytes accessed | tf_op | source)
XLA Modules:
  0.0 65.0 jit_solution(1598264980496548352)
XLA Ops:
  0.7 0.0 copy-start
  0.7 0.0 copy-start.1
  0.7 60.9 %shard_map.84 = (bf16[1,16,4,8,192]{4,3,2,1,0:T(8,128)(2,1)}, f32[480,128]{1,0:T(8,128)}) custom-call(bf16[1,16,4,8,192]{4,3,2,1,0:T(8,128)(2,1)} %x_hbm.1, bf16[1,16,4,8,192]{4,3,2,1,0:T(8,128)(2,1)} %cot_hbm.1, bf16[15552,192]{1,0:T(8,128)(2,1)} %bitcast.3), custom_call_target="tpu_custom_call" | custom-call | flops 8999999488 | bytes 10000000 | tf_op jit(solution)/shard_map/pallas_call | solution.py:510
  61.6 0.0 copy-done
  61.6 0.0 copy-done.1
  61.6 1.7 %add_divide_fusion = (f32[23328]{0:T(1024)}, f32[23328]{0:T(1024)}, f32[23328]{0:T(1024)}) fusion(f32[61440]{0:T(1024)} %bitcast.2, s32[]{:T(128)S(6)} %select_n.13, f32[23328]{0:T(1024)S(1)} %copy-done, f32[23328]{0:T(1024)S(1)} %copy-done.1), kind=kLoop, calls=%fused_computation | loop fusion | flops 279936 | bytes 559876 | tf_op jit(solution)/shard_map/div | solution.py:575
  63.4 1.7 %copy.10 = bf16[1,16,4,8,192]{4,3,2,1,0:T(8,128)(2,1)} copy(bf16[1,16,4,8,192]{4,3,2,1,0:T(8,128)(2,1)} %get-tuple-element.15) | data formatting | bytes 393216
Async XLA Ops:
  0.7 60.9 %copy-start = (f32[23328]{0:T(1024)S(1)}, f32[23328]{0:T(1024)}, u32[]{:S(2)}) copy-start(f32[23328]{0:T(1024)} %param.9) | copy-start | bytes 279940
  0.7 60.9 %copy-start.1 = (f32[23328]{0:T(1024)S(1)}, f32[23328]{0:T(1024)}, u32[]{:S(2)}) copy-start(f32[23328]{0:T(1024)} %param.8) | copy-start | bytes 279940

commit v8 on v7

--- a/solution.py
+++ b/solution.py
@@ -249,12 +249,13 @@
             device_id_type=MESH,
         )
 
-    def start(self, now):
+    def start(self, now, far):
         for target, a in self.spans:
             if a == now:
                 slot = lax.rem(self.me + 3 - target, 4)
-
-                @pl.when(self.me != target)
+                chosen = slot == 1 if far else (slot == 0) | (slot == 2)
+
+                @pl.when(chosen)
                 def _():
                     self.copy(target, a, slot).start()
 
@@ -378,12 +379,14 @@
             at = pl.ds((q // 4) * 5, 5)
             first_c[q % 4, at] = both_cores(2, window(1, q, 5), 5)
 
-        scatters[2].start(a)
+        scatters[2].start(a, False)
         for plane in (1, 0):
             for target, at, start, count in pieces(plane):
                 if ready(start, count) == a:
                     firsts[plane][target, at : at + count] = both_cores(plane, start, count)
-            scatters[plane].start(a)
+            scatters[plane].start(a, False)
+        for plane in (2, 1, 0):
+            scatters[plane].start(a, True)
 
     def input_terms(view_row, first):
         rim(gp, 1, view_row)

time: 65.2 us -> 65.6 us (level)
  no operation moved by 1% of the time
where the time goes in v8:
time: 65.6 us; the launch traced here: 65.4 us
  Pallas kernels  61.3 us (93%)
  other arithmetic  1.73 us (3%)
  local copies, waits for them, and re-layouts  1.68 us (3%)
  between operations  0.72 us (1%)
    pallas_call x1, Pallas kernels, local(): pl.pallas_call(step_kernel, out_shape=(jax.ShapeDtypeStruct(inputs.shape,...  61.3 us
    div x1, other arithmetic, local(): moment_next / first_fix / (jnp.sqrt(square_next / second_fix) + epsilon)  1.73 us
    unnamed x5, local copies, waits for them, and re-layouts  1.68 us

profile of v8, /device:TPU:1, one launch (start us, length us, event | category | flops | bytes accessed | tf_op | source)
XLA Modules:
  0.0 65.4 jit_solution(11366551119086707079)
XLA Ops:
  0.7 0.0 copy-start
  0.7 0.0 copy-start.1
  0.7 61.3 %shard_map.84 = (bf16[1,16,4,8,192]{4,3,2,1,0:T(8,128)(2,1)}, f32[480,128]{1,0:T(8,128)}) custom-call(bf16[1,16,4,8,192]{4,3,2,1,0:T(8,128)(2,1)} %x_hbm.1, bf16[1,16,4,8,192]{4,3,2,1,0:T(8,128)(2,1)} %cot_hbm.1, bf16[15552,192]{1,0:T(8,128)(2,1)} %bitcast.3), custom_call_target="tpu_custom_call" | custom-call | flops 8999999488 | bytes 10000000 | tf_op jit(solution)/shard_map/pallas_call | solution.py:513
  62.0 0.0 copy-done
  62.0 0.0 copy-done.1
  62.0 1.7 %add_divide_fusion = (f32[23328]{0:T(1024)}, f32[23328]{0:T(1024)}, f32[23328]{0:T(1024)}) fusion(f32[61440]{0:T(1024)} %bitcast.2, s32[]{:T(128)S(6)} %select_n.13, f32[23328]{0:T(1024)S(1)} %copy-done, f32[23328]{0:T(1024)S(1)} %copy-done.1), kind=kLoop, calls=%fused_computation | loop fusion | flops 279936 | bytes 559876 | tf_op jit(solution)/shard_map/div | solution.py:578
  63.8 1.7 %copy.10 = bf16[1,16,4,8,192]{4,3,2,1,0:T(8,128)(2,1)} copy(bf16[1,16,4,8,192]{4,3,2,1,0:T(8,128)(2,1)} %get-tuple-element.15) | data formatting | bytes 393216
Async XLA Ops:
  0.7 61.4 %copy-start = (f32[23328]{0:T(1024)S(1)}, f32[23328]{0:T(1024)}, u32[]{:S(2)}) copy-start(f32[23328]{0:T(1024)} %param.9) | copy-start | bytes 279940
  0.7 61.4 %copy-start.1 = (f32[23328]{0:T(1024)S(1)}, f32[23328]{0:T(1024)}, u32[]{:S(2)}) copy-start(f32[23328]{0:T(1024)} %param.8) | copy-start | bytes 279940

commit v9 on v4

--- a/solution.py
+++ b/solution.py
@@ -317,12 +317,14 @@
 
     wcopy.wait()
 
-    @pl.loop(0, 81)
-    def _(tap):
-        src = pl.ds(pl.multiple_of((80 - tap) * C, 64), C)
-        dst = pl.ds(pl.multiple_of(tap * C, 64), C)
-        wt[dst, :] = wv[src, :].T
-
+    def turn(low, high):
+        @pl.loop(low, high)
+        def _(tap):
+            src = pl.ds(pl.multiple_of((80 - tap) * C, 64), C)
+            dst = pl.ds(pl.multiple_of(tap * C, 64), C)
+            wt[dst, :] = wv[src, :].T
+
+    turn(0, 54)
     for copy, _, got in jobs[:2]:
         pl.when(got)(copy.wait_recv)
     rim(xp, 0, 1)
@@ -393,6 +395,7 @@
         kernel_terms(xc, gall, dw, a)
         pairs.append(exchange(a))
         scatter(pairs[a - 1], a - 1)
+    turn(54, 81)
     for copy, _, got in jobs[:2]:
         pl.when(got)(copy.wait_recv)
     input_terms(1, True)

time: 64 us -> 64.8 us (1.012)
  Pallas kernels: 59.7 us -> 60.5 us
    pallas_call x1, Pallas kernels: 59.7 us -> 60.5 us  [local(): pl.pallas_call(step_kernel, out_shape=(jax.ShapeDtypeStruct(inputs.shape,...]
where the time goes in v9:
time: 64.8 us; the launch traced here: 64.7 us
  Pallas kernels  60.5 us (93%)
  other arithmetic  1.73 us (3%)
  local copies, waits for them, and re-layouts  1.68 us (3%)
  between operations  0.72 us (1%)
    pallas_call x1, Pallas kernels, local(): pl.pallas_call(step_kernel, out_shape=(jax.ShapeDtypeStruct(inputs.shape,...  60.5 us
    div x1, other arithmetic, local(): moment_next / first_fix / (jnp.sqrt(square_next / second_fix) + epsilon)  1.73 us
    unnamed x5, local copies, waits for them, and re-layouts  1.68 us

profile of v9, /device:TPU:1, one launch (start us, length us, event | category | flops | bytes accessed | tf_op | source)
XLA Modules:
  0.0 64.7 jit_solution(10609502740699685894)
XLA Ops:
  0.7 0.0 copy-start
  0.7 0.0 copy-start.1
  0.7 60.5 %shard_map.84 = (bf16[1,16,4,8,192]{4,3,2,1,0:T(8,128)(2,1)}, f32[480,128]{1,0:T(8,128)}) custom-call(bf16[1,16,4,8,192]{4,3,2,1,0:T(8,128)(2,1)} %x_hbm.1, bf16[1,16,4,8,192]{4,3,2,1,0:T(8,128)(2,1)} %cot_hbm.1, bf16[15552,192]{1,0:T(8,128)(2,1)} %bitcast.3), custom_call_target="tpu_custom_call" | custom-call | flops 8999999488 | bytes 10000000 | tf_op jit(solution)/shard_map/pallas_call | solution.py:506
  61.2 0.0 copy-done
  61.2 0.0 copy-done.1
  61.3 1.7 %add_divide_fusion = (f32[23328]{0:T(1024)}, f32[23328]{0:T(1024)}, f32[23328]{0:T(1024)}) fusion(f32[61440]{0:T(1024)} %bitcast.2, s32[]{:T(128)S(6)} %select_n.13, f32[23328]{0:T(1024)S(1)} %copy-done, f32[23328]{0:T(1024)S(1)} %copy-done.1), kind=kLoop, calls=%fused_computation | loop fusion | flops 279936 | bytes 559876 | tf_op jit(solution)/shard_map/div | solution.py:571
  63.0 1.7 %copy.10 = bf16[1,16,4,8,192]{4,3,2,1,0:T(8,128)(2,1)} copy(bf16[1,16,4,8,192]{4,3,2,1,0:T(8,128)(2,1)} %get-tuple-element.15) | data formatting | bytes 393216
Async XLA Ops:
  0.7 60.6 %copy-start = (f32[23328]{0:T(1024)S(1)}, f32[23328]{0:T(1024)}, u32[]{:S(2)}) copy-start(f32[23328]{0:T(1024)} %param.9) | copy-start | bytes 279940
  0.7 60.6 %copy-start.1 = (f32[23328]{0:T(1024)S(1)}, f32[23328]{0:T(1024)}, u32[]{:S(2)}) copy-start(f32[23328]{0:T(1024)} %param.8) | copy-start | bytes 279940
